TPU v7x, 32 devices: a whole 2x2x4 slice. The times are simulated.
32 devices in a mesh: task: 4 (over y, core), fsdp: 8 (over z, x).
Axes of the slice: x: 2, y: 2, z: 4, core: 2. Of those that a mesh axis runs over, the one named last changes fastest.
Arguments:
- stitch: float32 [4, 4], replicated, may hold values from -3 to 3
- out_grad: bfloat16 [4, 4096, 1792], P('task', 'fsdp'), may hold values from -6 to 6
- block_out: bfloat16 [4, 4096, 1792], P('task', 'fsdp'), may hold values from -6 to 6
- queries: bfloat16 [4, 4096, 1792], P('task', 'fsdp'), may hold values from -80 to 80
- key_rows: bfloat16 [4, 4096, 1792], P('task', 'fsdp'), may hold values from -4 to 4
- values: bfloat16 [4, 4096, 1792], P('task', 'fsdp'), may hold values from -6 to 6
- out_proj: bfloat16 [4, 1792, 1792], P('task', 'fsdp'), may hold values from -0.125 to 0.125
Outputs:
- residual_grad: bfloat16 [4, 4096, 1792], P('task', 'fsdp')
- query_grad: bfloat16 [4, 4096, 1792], P('task', 'fsdp')
- key_grad: bfloat16 [4, 4096, 1792], P('task', 'fsdp')
- value_grad: bfloat16 [4, 4096, 1792], P('task', 'fsdp')
- proj_grad: float32 [4, 1792, 1792], P('task', 'fsdp')
- stitch_grad: float32 [4, 4], P('task')
All inputs are finite; a program needn't handle non-finite values.
Results may differ from a plain program's by a relative error of at most 0.0066.
Values may be sent and summed in bfloat16 or wider, within the bound.
A program may use at most 192 MiB of HBM per device.

v0:
```python
import functools
import math

import jax
import jax.numpy as jnp
from jax import lax
from jax.experimental import pallas as pl
from jax.experimental.pallas import tpu as pltpu
from jax.sharding import PartitionSpec as P

HEADS = 16
HEAD = 112
PATCHES = 256
GROUP = 8
FACTOR = 1.0 / math.sqrt(HEAD)
CORES = 2
VMEM = 40 * 1024 * 1024


def dot(a, b, ca, cb):
    return lax.dot_general(a, b, (((ca,), (cb,)), ((), ())), preferred_element_type=jnp.float32)


def softmax(q, k):
    scores = dot(q, k, 1, 1) * FACTOR
    weights = jnp.exp(scores - jnp.max(scores, axis=-1, keepdims=True))
    return weights, 1.0 / jnp.sum(weights, axis=-1, keepdims=True)


def forward_kernel(q_ref, k_ref, v_ref, o_ref):
    for head in range(GROUP):
        cols = slice(head * HEAD, (head + 1) * HEAD)
        weights, inverse = softmax(q_ref[:, cols], k_ref[:, cols])
        probs_b = (weights * inverse).astype(jnp.bfloat16)
        o_ref[:, cols] = dot(probs_b, v_ref[:, cols], 1, 0).astype(jnp.bfloat16)


def backward_kernel(q_ref, k_ref, v_ref, g_ref, dq_ref, dk_ref, dv_ref):
    for head in range(GROUP):
        cols = slice(head * HEAD, (head + 1) * HEAD)
        q, k, v, g = q_ref[:, cols], k_ref[:, cols], v_ref[:, cols], g_ref[:, cols]
        weights, inverse = softmax(q, k)
        probs = weights * inverse
        dprobs = dot(g, v, 1, 1)
        row_dots = jnp.sum(probs * dprobs, axis=-1, keepdims=True)
        dscores = (probs * (dprobs - row_dots) * FACTOR).astype(jnp.bfloat16)
        dq_ref[:, cols] = dot(dscores, k, 1, 0).astype(jnp.bfloat16)
        dk_ref[:, cols] = dot(dscores, q, 0, 0).astype(jnp.bfloat16)
        dv_ref[:, cols] = dot(probs.astype(jnp.bfloat16), g, 0, 0).astype(jnp.bfloat16)


def attention_call(kernel, outputs, matmuls, exps, *arrays):
    rows, features = arrays[0].shape
    width = GROUP * HEAD
    spec = pl.BlockSpec((PATCHES, width), lambda i, j: (i, j))
    shape = jax.ShapeDtypeStruct((rows, features), jnp.bfloat16)
    return pl.pallas_call(
        kernel,
        grid=(rows // PATCHES, features // width),
        in_specs=[spec] * len(arrays),
        out_specs=[spec] * outputs,
        out_shape=[shape] * outputs,
        compiler_params=pltpu.CompilerParams(vmem_limit_bytes=VMEM),
        cost_estimate=pl.CostEstimate(
            flops=matmuls * 2 * rows * PATCHES * features,
            bytes_accessed=2 * rows * features * (len(arrays) + outputs),
            transcendentals=rows * PATCHES * HEADS * exps,
        ),
    )(*arrays)


def stitch_kernel(towers, coef_ref, own_ref, *refs):
    pieces, (res_ref, dots_ref) = refs[:towers], refs[towers:]

    @pl.when(pl.program_id(0) == 0)
    def _():
        dots_ref[...] = jnp.zeros_like(dots_ref)

    own = own_ref[...].astype(jnp.float32)
    mixed = jnp.zeros_like(own)
    for j in range(towers):
        piece = pieces[j][...].astype(jnp.float32)
        mixed = mixed + coef_ref[0, j] * piece
        dots_ref[j : j + 1, :] += jnp.sum(piece * own, axis=0, keepdims=True)
    res_ref[...] = mixed.astype(jnp.bfloat16)


def stitch_call(coefs, own, pieces):
    rows, features = own.shape
    towers = len(pieces)
    step = 64
    spec = pl.BlockSpec((step, features), lambda i: (i, 0))
    return pl.pallas_call(
        functools.partial(stitch_kernel, towers),
        grid=(rows // step,),
        in_specs=[pl.BlockSpec(memory_space=pltpu.SMEM)] + [spec] * (towers + 1),
        out_specs=[spec, pl.BlockSpec((towers, features), lambda i: (0, 0))],
        out_shape=[
            jax.ShapeDtypeStruct((rows, features), jnp.bfloat16),
            jax.ShapeDtypeStruct((towers, features), jnp.float32),
        ],
        compiler_params=pltpu.CompilerParams(vmem_limit_bytes=VMEM),
        cost_estimate=pl.CostEstimate(
            flops=4 * rows * features * towers,
            bytes_accessed=2 * rows * features * (towers + 2),
            transcendentals=0,
        ),
    )(coefs, own, *pieces)


def tower_pieces(piece, towers, tower):
    chips = towers // CORES
    chip, core = tower // CORES, tower % CORES
    swap = [(t, t ^ 1) for t in range(towers)]
    same, owners = [piece], [tower]
    for shift in range(1, chips):
        perm = [(t, (t + CORES * shift) % towers) for t in range(towers)]
        same.append(lax.ppermute(piece, "task", perm))
        owners.append((chip - shift + chips) % chips * CORES + core)
    crossed = [lax.ppermute(block, "task", swap) for block in same]
    return same + crossed, owners + [owner + 1 - 2 * core for owner in owners]


def body(stitch, out_grad, block_out, queries, key_rows, values, out_proj):
    tower = lax.axis_index("task")
    towers = lax.axis_size("task")
    count_shards = lax.axis_size("fsdp")
    tok_rows = out_grad.shape[1]
    weight = lax.all_gather(out_proj, "fsdp", axis=1, tiled=True)[0]
    pieces, owners = tower_pieces(out_grad[0], towers, tower)
    owners = jnp.stack(owners)
    here = owners[:, None] == jnp.arange(towers)[None, :]
    column = lax.dynamic_slice_in_dim(stitch, tower, 1, 1)[:, 0]
    coefs = jnp.sum(jnp.where(here, column[None, :], 0.0), axis=1)[None, :]

    (attended,) = attention_call(forward_kernel, 1, 2, 1, queries[0], key_rows[0], values[0])
    residual, dots = stitch_call(coefs, block_out[0], pieces)
    share = lax.dot_general(
        attended, residual, (((0,), (0,)), ((), ())), preferred_element_type=jnp.float32
    ).astype(jnp.bfloat16)
    proj_grad = lax.psum_scatter(share, "fsdp", scatter_dimension=0, tiled=True)

    sums = jnp.sum(dots, axis=1)
    sums = jnp.sum(jnp.where(here, sums[:, None], 0.0), axis=0)[None, :]
    hop = 1
    while hop < count_shards:
        sums = sums + lax.ppermute(sums, "fsdp", [(d, d ^ hop) for d in range(count_shards)])
        hop *= 2
    stitch_grad = sums / (tok_rows * count_shards)

    attended_grad = lax.dot_general(
        residual, weight, (((1,), (1,)), ((), ())), preferred_element_type=jnp.float32
    ).astype(jnp.bfloat16)
    query_out, key_out, value_out = attention_call(
        backward_kernel, 3, 6, 1, queries[0], key_rows[0], values[0], attended_grad
    )
    return (
        residual[None],
        query_out[None],
        key_out[None],
        value_out[None],
        proj_grad.astype(jnp.float32)[None],
        stitch_grad,
    )


def solution(mesh):
    rows = P("task", "fsdp", None)
    return jax.shard_map(
        body,
        mesh=mesh,
        in_specs=(P(), rows, rows, rows, rows, rows, rows),
        out_specs=(rows, rows, rows, rows, rows, P("task", None)),
        check_vma=False,
    )
```

profile of v0, /device:TPU:0, one launch (start us, length us, event | category | flops | bytes accessed | tf_op | source)
XLA Modules:
  0.0 244.5 jit_solution(12550442301090012533)
XLA Ops:
  7.2 0.7 all-gather.2.cloned.1.call-update
  8.0 3.0 %collective-permute-start = (bf16[512,1792]{1,0:T(8,128)(2,1)}, bf16[512,1792]{1,0:T(8,128)(2,1)S(1)}, u32[]{:S(2)}, u32[]{:S(2)}) collective-permute-start(bf16[512,1792]{1,0:T(8,128)(2,1)} %bitcast.28), channel_id=1, source_target_pairs={{0,16},{8,24},{16,0},{24,8},{1,17},{9,25},{17,1},{25,9},{2,18},{10... | collective-permute-start | bytes 5505032 | tf_op jit(solution)/shard_map/ppermute | solution.py:118
  11.0 40.2 %collective-permute-done.refs_1_ = bf16[512,1792]{1,0:T(8,128)(2,1)S(1)} collective-permute-done((bf16[512,1792]{1,0:T(8,128)(2,1)}, bf16[512,1792]{1,0:T(8,128)(2,1)S(1)}, u32[]{:S(2)}, u32[]{:S(2)}) %collective-permute-start) | collective-permute-done | bytes 1835040 | tf_op jit(solution)/shard_map/ppermute | solution.py:118
  51.2 0.2 dynamic-slice_reduce_fusion
  51.4 1.5 copy-done.3
  52.9 1.5 copy-done.5
  54.4 1.5 copy-done.7
  55.9 15.6 %shard_map.120 = bf16[512,1792]{1,0:T(8,128)(2,1)S(1)} custom-call(bf16[512,1792]{1,0:T(8,128)(2,1)S(1)} %bitcast.31, bf16[512,1792]{1,0:T(8,128)(2,1)S(1)} %bitcast.33, bf16[512,1792]{1,0:T(8,128)(2,1)S(1)} %bitcast.35), custom_call_target="tpu_custom_call" | custom-call | flops 939524096 | bytes 7340032 | tf_op jit(solution)/shard_map/pallas_call | solution.py:57
  71.6 0.2 select_reduce_fusion.1
  71.9 7.2 %shard_map.118 = (bf16[512,1792]{1,0:T(8,128)(2,1)}, f32[4,1792]{1,0:T(4,128)S(1)}) custom-call(f32[1,4]{1,0:T(1,128)S(1)} %bitcast.37, bf16[512,1792]{1,0:T(8,128)(2,1)S(1)} %bitcast.27, bf16[512,1792]{1,0:T(8,128)(2,1)S(1)} %bitcast.30, bf16[512,1792]{1,0:T(8,128)(2,1)S(1)} %collective-permute-done.refs_1_, ...), custom_call_target="tpu_custom_call" | custom-call | flops 14680064 | bytes 11010048 | tf_op jit(solution)/shard_map/pallas_call | solution.py:93
  79.0 7.0 %convolution_convert_fusion = bf16[1792,1792]{1,0:T(8,128)(2,1)} fusion(bf16[512,1792]{1,0:T(8,128)(2,1)S(1)} %shard_map.120, bf16[512,1792]{1,0:T(8,128)(2,1)} %get-tuple-element.11), kind=kOutput, calls=%fused_computation | convolution fusion | flops 3291545600 | bytes 10092544 | tf_op jit(solution)/shard_map/dot_general | solution.py:138
  86.0 0.1 reduce_sum.28
  86.2 1.7 collective-permute-start.3
  88.0 1.8 collective-permute-done.3
  89.8 1.8 collective-permute-start.4
  91.6 1.8 collective-permute-done.4
  93.4 2.8 %collective-permute-start.5 = (f32[1,4]{1,0:T(1,128)S(1)}, f32[1,4]{1,0:T(1,128)S(1)}, u32[]{:S(2)}, u32[]{:S(2)}) collective-permute-start(f32[1,4]{1,0:T(1,128)S(1)} %add.45), channel_id=1, source_target_pairs={{0,4},{1,5},{2,6},{3,7},{4,0},{5,1},{6,2},{7,3},{8,12},{9,13},{10,... | collective-permute-start | bytes 56 | tf_op jit(solution)/shard_map/ppermute | solution.py:147
  96.2 2.3 collective-permute-done.5
  98.4 0.5 add_multiply_fusion
  98.9 14.6 %all-gather.2.cloned.1.call-done = bf16[1,1792,1792]{2,1,0:T(8,128)(2,1)} async-done(((bf16[1,224,1792]{2,1,0:T(8,128)(2,1)}), bf16[1,1792,1792]{2,1,0:T(8,128)(2,1)}) %all-gather.2.cloned.1.call-update) | async-done | bytes 6422544 | tf_op jit(solution)/shard_map/all_gather | solution.py:129
  113.6 7.0 %fusion.2.g_ref = bf16[512,1792]{1,0:T(8,128)(2,1)S(1)} fusion(bf16[512,1792]{1,0:T(8,128)(2,1)} %get-tuple-element.11, bf16[1,1792,1792]{2,1,0:T(8,128)(2,1)} %all-gather.2.cloned.1.call-done), kind=kOutput, calls=%fused_computation.3 | convolution fusion | flops 3289251840 | bytes 10092544 | tf_op jit(solution)/shard_map/dot_general | solution.py:151
  120.7 24.0 %shard_map.119 = (bf16[512,1792]{1,0:T(8,128)(2,1)}, bf16[512,1792]{1,0:T(8,128)(2,1)}, bf16[512,1792]{1,0:T(8,128)(2,1)}) custom-call(bf16[512,1792]{1,0:T(8,128)(2,1)S(1)} %bitcast.32, bf16[512,1792]{1,0:T(8,128)(2,1)S(1)} %bitcast.34, bf16[512,1792]{1,0:T(8,128)(2,1)S(1)} %bitcast.36, bf16[512,1792]{1,0:T(8,128)(2,1)S(1)} %fusion.2.g_ref), custom_call_target="tpu_custom_call" | custom-call | flops 2818572288 | bytes 12845056 | tf_op jit(solution)/shard_map/pallas_call | solution.py:57
  144.7 90.6 %reduce-scatter.2.cloned.1.call-done = bf16[224,1792]{1,0:T(8,128)(2,1)} async-done(((bf16[1792,1792]{1,0:T(8,128)(2,1)}), bf16[224,1792]{1,0:T(8,128)(2,1)}) %reduce-scatter.2.cloned.1.call-update) | async-done | bytes 802832 | tf_op jit(solution)/shard_map/reduce_scatter | solution.py:141
  235.2 2.4 bitcast_convert_fusion
  (26 shorter events, 0.3 us)
Async XLA Ops:
  7.2 44.1 %copy-start = (f32[4,4]{1,0:T(4,128)S(1)}, f32[4,4]{1,0:T(4,128)}, u32[]{:S(2)}) copy-start(f32[4,4]{1,0:T(4,128)} %param.7) | copy-start | bytes 196
  7.2 106.4 %all-gather.2.cloned.1.call-start = ((), (), s32[]{:S(2)}) async-start(), calls=%async_computation.1 | async-start | bytes 7225344 | tf_op jit(solution)/shard_map/all_gather | solution.py:129
  7.9 227.3 %reduce-scatter.2.cloned.1.call-start = ((), (), s32[]{:S(2)}) async-start(), calls=%async_computation.2 | async-start | bytes 7225344 | tf_op jit(solution)/shard_map/reduce_scatter | solution.py:141
  8.0 43.3 %collective-permute-start = (bf16[512,1792]{1,0:T(8,128)(2,1)}, bf16[512,1792]{1,0:T(8,128)(2,1)S(1)}, u32[]{:S(2)}, u32[]{:S(2)}) collective-permute-start(bf16[512,1792]{1,0:T(8,128)(2,1)} %bitcast.28), channel_id=1, source_target_pairs={{0,16},{8,24},{16,0},{24,8},{1,17},{9,25},{17,1},{25,9},{2,18},{10... | collective-permute-start | bytes 5505032 | tf_op jit(solution)/shard_map/ppermute | solution.py:118
  11.0 60.8 %collective-permute-start.1 = (bf16[512,1792]{1,0:T(8,128)(2,1)}, bf16[512,1792]{1,0:T(8,128)(2,1)}, u32[]{:S(2)}, u32[]{:S(2)}) collective-permute-start(bf16[512,1792]{1,0:T(8,128)(2,1)} %bitcast.29), channel_id=1, source_target_pairs={{0,8},{8,0},{16,24},{24,16},{1,9},{9,1},{17,25},{25,17},{2,10},{10... | collective-permute-start | bytes 5505032 | tf_op jit(solution)/shard_map/ppermute | solution.py:120
  51.2 20.6 %collective-permute-start.2 = (bf16[512,1792]{1,0:T(8,128)(2,1)S(1)}, bf16[512,1792]{1,0:T(8,128)(2,1)}, u32[]{:S(2)}, u32[]{:S(2)}) collective-permute-start(bf16[512,1792]{1,0:T(8,128)(2,1)S(1)} %collective-permute-done.refs_1_), channel_id=1, source_target_pairs={{0,8},{8,0},{16,24},{24,16},{1,9},{9,1},{17,25},{25,17},{2,10},{10... | collective-permute-start | bytes 5505032 | tf_op jit(solution)/shard_map/ppermute | solution.py:120
  51.4 1.5 copy-start.3
  52.9 1.5 copy-start.5
  54.4 1.5 copy-start.7
  55.9 15.9 %copy-start.1 = (bf16[1,512,1792]{2,1,0:T(8,128)(2,1)S(1)}, bf16[1,512,1792]{2,1,0:T(8,128)(2,1)}, u32[]{:S(2)}) copy-start(bf16[1,512,1792]{2,1,0:T(8,128)(2,1)} %param.9) | copy-start | bytes 5505028
  55.9 15.9 %copy-start.2 = (bf16[1,512,1792]{2,1,0:T(8,128)(2,1)S(1)}, bf16[1,512,1792]{2,1,0:T(8,128)(2,1)}, u32[]{:S(2)}) copy-start(bf16[1,512,1792]{2,1,0:T(8,128)(2,1)} %param.8) | copy-start | bytes 5505028
  86.2 3.6 %collective-permute-start.3 = (f32[1,4]{1,0:T(1,128)S(1)}, f32[1,4]{1,0:T(1,128)S(1)}, u32[]{:S(2)}, u32[]{:S(2)}) collective-permute-start(f32[1,4]{1,0:T(1,128)S(1)} %bitcast.39), channel_id=1, source_target_pairs={{0,1},{1,0},{2,3},{3,2},{4,5},{5,4},{6,7},{7,6},{8,9},{9,8},{10,11... | collective-permute-start | bytes 56 | tf_op jit(solution)/shard_map/ppermute | solution.py:147
  89.8 3.6 %collective-permute-start.4 = (f32[1,4]{1,0:T(1,128)S(1)}, f32[1,4]{1,0:T(1,128)S(1)}, u32[]{:S(2)}, u32[]{:S(2)}) collective-permute-start(f32[1,4]{1,0:T(1,128)S(1)} %bitcast_add_fusion), channel_id=1, source_target_pairs={{0,2},{1,3},{2,0},{3,1},{4,6},{5,7},{6,4},{7,5},{8,10},{9,11},{10,... | collective-permute-start | bytes 56 | tf_op jit(solution)/shard_map/ppermute | solution.py:147
  93.4 5.0 %collective-permute-start.5 = (f32[1,4]{1,0:T(1,128)S(1)}, f32[1,4]{1,0:T(1,128)S(1)}, u32[]{:S(2)}, u32[]{:S(2)}) collective-permute-start(f32[1,4]{1,0:T(1,128)S(1)} %add.45), channel_id=1, source_target_pairs={{0,4},{1,5},{2,6},{3,7},{4,0},{5,1},{6,2},{7,3},{8,12},{9,13},{10,... | collective-permute-start | bytes 56 | tf_op jit(solution)/shard_map/ppermute | solution.py:147
  98.9 21.7 %copy-start.4 = (bf16[1,512,1792]{2,1,0:T(8,128)(2,1)S(1)}, bf16[1,512,1792]{2,1,0:T(8,128)(2,1)}, u32[]{:S(2)}) copy-start(bf16[1,512,1792]{2,1,0:T(8,128)(2,1)} %param.10) | copy-start | bytes 5505028
  113.6 7.1 %copy-start.6 = (bf16[1,512,1792]{2,1,0:T(8,128)(2,1)S(1)}, bf16[1,512,1792]{2,1,0:T(8,128)(2,1)}, u32[]{:S(2)}) copy-start(bf16[1,512,1792]{2,1,0:T(8,128)(2,1)} %param.11) | copy-start | bytes 5505028
  113.6 7.1 %copy-start.8 = (bf16[1,512,1792]{2,1,0:T(8,128)(2,1)S(1)}, bf16[1,512,1792]{2,1,0:T(8,128)(2,1)}, u32[]{:S(2)}) copy-start(bf16[1,512,1792]{2,1,0:T(8,128)(2,1)} %param.12) | copy-start | bytes 5505028
Sparse Core Ops, SparseCore 0:
  10.2 103.3 all-gather.1
  117.2 118.0 reduce-scatter.1
where the time goes:
time: 245 us; the launch traced here: 244 us
  waiting for transfers between devices  152 us (62%)
  Pallas kernels  46.8 us (19%)
  between operations  14.1 us (6%)
  matrix products  14 us (6%)
  starting transfers between devices  9.41 us (4%)
  local copies, waits for them, and re-layouts  4.71 us (2%)
  other arithmetic  3.4 us (1%)
    reduce_scatter x1, waiting for transfers between devices, body(): proj_grad = lax.psum_scatter(share, 'fsdp', scatter_dimension=0, tiled=True)  90.6 us
    ppermute x1, waiting for transfers between devices, tower_pieces(): same.append(lax.ppermute(piece, 'task', perm))  40.2 us
    pallas_call x2, Pallas kernels, attention_call(): pl.pallas_call(kernel, grid=(rows // PATCHES, features // width), in_spec...  39.7 us
    all_gather x1, waiting for transfers between devices, body(): weight = lax.all_gather(out_proj, 'fsdp', axis=1, tiled=True)[0]  14.6 us
    pallas_call x1, Pallas kernels, stitch_call(): pl.pallas_call(functools.partial(stitch_kernel, towers), grid=(rows // st...  7.16 us
    dot_general x1, matrix products, body(): lax.dot_general(residual, weight, (((1,), (1,)), ((), ())), preferred_ele...  7.03 us
    dot_general x1, matrix products, body(): lax.dot_general(attended, residual, (((0,), (0,)), ((), ())), preferred_e...  6.96 us
    ppermute x3, starting transfers between devices, body(): lax.ppermute(sums, 'fsdp', [(d, d ^ hop) for d in range(count_shards)])  6.3 us
  transfers between devices with their start and end apart: 8, of which 6 were waited for; matrix products, arithmetic and copies ran while one was open for 6% of the time, Pallas kernels for 19%

commit v1 on v0

--- a/solution.py
+++ b/solution.py
@@ -15,6 +15,8 @@
 FACTOR = 1.0 / math.sqrt(HEAD)
 CORES = 2
 VMEM = 40 * 1024 * 1024
+OUTER = 4
+EARLY_X = 1152
 
 
 def dot(a, b, ca, cb):
@@ -108,7 +110,61 @@
     )(coefs, own, *pieces)
 
 
-def tower_pieces(piece, towers, tower):
+def wide(block):
+    return block.astype(jnp.float32)
+
+
+def sum_inner(block_for, inner, mine, shards):
+    total = wide(block_for(mine))
+    for shift in range(1, inner):
+        perm = [(d, d // inner * inner + (d + shift) % inner) for d in range(shards)]
+        total += wide(lax.ppermute(block_for((mine + shift) % inner), "fsdp", perm))
+    return total
+
+
+def sum_outer(block_at, inner, shards, then=None):
+    right = left = None
+    for far in range(OUTER - 1, 0, -1):
+        ahead, behind = wide(block_at(far)), wide(block_at(OUTER - far))
+        if right is not None:
+            ahead, behind = ahead + wide(right), behind + wide(left)
+        up = [(d, d + inner) for d in range(shards) if d // inner + far < OUTER]
+        down = [(d, d - inner) for d in range(shards) if d // inner >= far]
+        right = lax.ppermute(ahead.astype(jnp.bfloat16), "fsdp", up)
+        left = lax.ppermute(behind.astype(jnp.bfloat16), "fsdp", down)
+        if far > 1:
+            right, left = lax.optimization_barrier((right, left))
+        if far == 2 and then is not None:
+            right, left, *then[:] = lax.optimization_barrier((right, left, *then))
+    return wide(block_at(0)), right, left
+
+
+def scatter_sum(share, shards, then):
+    rows = share.shape[0] // shards
+    inner = shards // OUTER
+    place = lax.axis_index("fsdp")
+    far, near = place // inner, place % inner
+
+    def rows_of(array, start, size):
+        return lax.dynamic_slice_in_dim(array, start * rows, size * rows, 0)
+
+    first, second = share[:, :EARLY_X], share[:, EARLY_X:]
+    parts = [
+        sum_inner(
+            lambda i, o=(far + shift) % OUTER: rows_of(first, o * inner + i, 1), inner, near, shards
+        ).astype(jnp.bfloat16)
+        for shift in range(OUTER)
+    ]
+
+    own, right, left = sum_outer(
+        lambda shift: rows_of(second, (far + shift) % OUTER * inner, inner), inner, shards
+    )
+    line = (own + wide(right) + wide(left)).astype(jnp.bfloat16)
+    second_sum = sum_inner(lambda i: rows_of(line, i, 1), inner, near, shards)
+    return second_sum, sum_outer(lambda shift: parts[shift], inner, shards, then)
+
+
+def tower_pieces(piece, towers, tower, before):
     chips = towers // CORES
     chip, core = tower // CORES, tower % CORES
     swap = [(t, t ^ 1) for t in range(towers)]
@@ -117,8 +173,11 @@
         perm = [(t, (t + CORES * shift) % towers) for t in range(towers)]
         same.append(lax.ppermute(piece, "task", perm))
         owners.append((chip - shift + chips) % chips * CORES + core)
-    crossed = [lax.ppermute(block, "task", swap) for block in same]
-    return same + crossed, owners + [owner + 1 - 2 * core for owner in owners]
+    crossed = [lax.ppermute(piece, "task", swap)]
+    moved, before = lax.optimization_barrier((same[1:], before))
+    same = [piece] + moved
+    crossed += [lax.ppermute(block, "task", swap) for block in moved]
+    return before, same + crossed, owners + [owner + 1 - 2 * core for owner in owners]
 
 
 def body(stitch, out_grad, block_out, queries, key_rows, values, out_proj):
@@ -127,18 +186,20 @@
     count_shards = lax.axis_size("fsdp")
     tok_rows = out_grad.shape[1]
     weight = lax.all_gather(out_proj, "fsdp", axis=1, tiled=True)[0]
-    pieces, owners = tower_pieces(out_grad[0], towers, tower)
+    (attended,) = attention_call(forward_kernel, 1, 2, 1, queries[0], key_rows[0], values[0])
+    attended, pieces, owners = tower_pieces(out_grad[0], towers, tower, attended)
     owners = jnp.stack(owners)
     here = owners[:, None] == jnp.arange(towers)[None, :]
     column = lax.dynamic_slice_in_dim(stitch, tower, 1, 1)[:, 0]
     coefs = jnp.sum(jnp.where(here, column[None, :], 0.0), axis=1)[None, :]
 
-    (attended,) = attention_call(forward_kernel, 1, 2, 1, queries[0], key_rows[0], values[0])
     residual, dots = stitch_call(coefs, block_out[0], pieces)
     share = lax.dot_general(
         attended, residual, (((0,), (0,)), ((), ())), preferred_element_type=jnp.float32
     ).astype(jnp.bfloat16)
-    proj_grad = lax.psum_scatter(share, "fsdp", scatter_dimension=0, tiled=True)
+    held = [weight]
+    second_sum, (own, right, left) = scatter_sum(share, count_shards, held)
+    (weight,) = held
 
     sums = jnp.sum(dots, axis=1)
     sums = jnp.sum(jnp.where(here, sums[:, None], 0.0), axis=0)[None, :]
@@ -154,12 +215,16 @@
     query_out, key_out, value_out = attention_call(
         backward_kernel, 3, 6, 1, queries[0], key_rows[0], values[0], attended_grad
     )
+    right, left, query_out, key_out, value_out = lax.optimization_barrier(
+        (right, left, query_out, key_out, value_out)
+    )
+    proj_grad = jnp.concatenate([own + wide(right) + wide(left), second_sum], axis=1)
     return (
         residual[None],
         query_out[None],
         key_out[None],
         value_out[None],
-        proj_grad.astype(jnp.float32)[None],
+        proj_grad[None],
         stitch_grad,
     )
 

time: 245 us -> 223 us (0.910)
  waiting for transfers between devices: 152 us -> 59 us
  starting transfers between devices: 9.41 us -> 58.5 us
  local copies, waits for them, and re-layouts: 4.71 us -> 18.4 us
  other arithmetic: 3.4 us -> 13.6 us
    reduce_scatter x1 -> x0, waiting for transfers between devices: 90.6 us -> none  [body(): proj_grad = lax.psum_scatter(share, 'fsdp', scatter_dimension=0, tiled=True)]
    ppermute x2 -> x19, starting transfers between devices: 0.01 us -> 42.1 us  [the longest x6 28.1 us: sum_outer(): right = lax.ppermute(ahead.astype(jnp.bfloat16), 'fsdp', up)]
    ppermute x2 -> x19, waiting for transfers between devices: 0.01 us -> 36.3 us  [the longest x6 29.6 us: sum_outer(): right = lax.ppermute(ahead.astype(jnp.bfloat16), 'fsdp', up)]
    ppermute x1, waiting for transfers between devices: 40.2 us -> 19 us  [tower_pieces(): same.append(lax.ppermute(piece, 'task', perm))]
    all_gather x1, waiting for transfers between devices: 14.6 us -> 0.02 us  [body(): weight = lax.all_gather(out_proj, 'fsdp', axis=1, tiled=True)[0]]
    convert_element_type x0 -> x8, other arithmetic: none -> 9.88 us  [the longest x4 5.35 us: sum_outer(): left = lax.ppermute(behind.astype(jnp.bfloat16), 'fsdp', down)]
    unnamed x18 -> x44, local copies, waits for them, and re-layouts: 4.52 us -> 14 us
    ppermute x3, starting transfers between devices: 6.3 us -> 13.2 us  [body(): lax.ppermute(sums, 'fsdp', [(d, d ^ hop) for d in range(count_shards)])]
  transfers between devices with their start and end apart: 8 -> 24, of which waited for: 6 -> 9; matrix products, arithmetic and copies ran while one was open for 6% -> 12% of each run, Pallas kernels for 19% -> 21%
where the time goes in v1:
time: 223 us
  waiting for transfers between devices  59 us (26%)
  starting transfers between devices  58.5 us (26%)
  Pallas kernels  47.1 us (21%)
  local copies, waits for them, and re-layouts  18.4 us (8%)
  between operations  14.4 us (6%)
  other arithmetic  13.6 us (6%)
  matrix products  11.7 us (5%)
    pallas_call x2, Pallas kernels, attention_call(): pl.pallas_call(kernel, grid=(rows // PATCHES, features // width), in_spec...  39.5 us
    ppermute x6, waiting for transfers between devices, sum_outer(): right = lax.ppermute(ahead.astype(jnp.bfloat16), 'fsdp', up)  29.6 us
    ppermute x6, starting transfers between devices, sum_outer(): right = lax.ppermute(ahead.astype(jnp.bfloat16), 'fsdp', up)  28.1 us
    ppermute x1, waiting for transfers between devices, tower_pieces(): same.append(lax.ppermute(piece, 'task', perm))  19 us
    unnamed x44, local copies, waits for them, and re-layouts  14 us
    ppermute x3, starting transfers between devices, body(): lax.ppermute(sums, 'fsdp', [(d, d ^ hop) for d in range(count_shards)])  13.2 us
    pallas_call x1, Pallas kernels, stitch_call(): pl.pallas_call(functools.partial(stitch_kernel, towers), grid=(rows // st...  7.59 us
    ppermute x6, starting transfers between devices, sum_outer(): left = lax.ppermute(behind.astype(jnp.bfloat16), 'fsdp', down)  7.18 us
  transfers between devices with their start and end apart: 24, of which 9 were waited for; matrix products, arithmetic and copies ran while one was open for 12% of the time, Pallas kernels for 21%

profile of v1, /device:TPU:0, one launch (start us, length us, event | category | flops | bytes accessed | tf_op | source)
XLA Modules:
  0.0 222.6 jit_solution(1551063904313851126)
XLA Ops:
  7.9 3.0 %collective-permute-start = (bf16[512,1792]{1,0:T(8,128)(2,1)}, bf16[512,1792]{1,0:T(8,128)(2,1)}, u32[]{:S(2)}, u32[]{:S(2)}) collective-permute-start(bf16[512,1792]{1,0:T(8,128)(2,1)} %bitcast.24), channel_id=1, source_target_pairs={{0,16},{8,24},{16,0},{24,8},{1,17},{9,25},{17,1},{25,9},{2,18},{10... | collective-permute-start | bytes 5505032 | tf_op jit(solution)/shard_map/ppermute | solution.py:174
  15.5 15.6 %shard_map.118 = bf16[512,1792]{1,0:T(8,128)(2,1)S(1)} custom-call(bf16[512,1792]{1,0:T(8,128)(2,1)S(1)} %bitcast.27, bf16[512,1792]{1,0:T(8,128)(2,1)S(1)} %bitcast.29, bf16[512,1792]{1,0:T(8,128)(2,1)S(1)} %bitcast.31), custom_call_target="tpu_custom_call" | custom-call | flops 939524096 | bytes 7340032 | tf_op jit(solution)/shard_map/pallas_call | solution.py:59
  32.3 19.0 %collective-permute-done.refs_1_ = bf16[512,1792]{1,0:T(8,128)(2,1)} collective-permute-done((bf16[512,1792]{1,0:T(8,128)(2,1)}, bf16[512,1792]{1,0:T(8,128)(2,1)}, u32[]{:S(2)}, u32[]{:S(2)}) %collective-permute-start) | collective-permute-done | bytes 1835040 | tf_op jit(solution)/shard_map/ppermute | solution.py:174
  51.7 3.7 %collective-permute-done.2.refs_3_ = bf16[512,1792]{1,0:T(8,128)(2,1)} collective-permute-done((bf16[512,1792]{1,0:T(8,128)(2,1)}, bf16[512,1792]{1,0:T(8,128)(2,1)}, u32[]{:S(2)}, u32[]{:S(2)}) %collective-permute-start.2) | collective-permute-done | bytes 1835040 | tf_op jit(solution)/shard_map/ppermute | solution.py:179
  55.4 1.9 copy-done.3
  57.3 7.6 %shard_map.119 = (bf16[512,1792]{1,0:T(8,128)(2,1)}, f32[4,1792]{1,0:T(4,128)S(1)}) custom-call(f32[1,4]{1,0:T(1,128)S(1)} %bitcast.33, bf16[512,1792]{1,0:T(8,128)(2,1)S(1)} %bitcast.23, bf16[512,1792]{1,0:T(8,128)(2,1)S(1)} %bitcast.26, bf16[512,1792]{1,0:T(8,128)(2,1)} %collective-permute-done.refs_1_, bf16[512,1792]{1,0:T(8,128)(2,1)} %collective-permute-done.1.refs_2_, ...), custom_call_target="tpu_custom_call" | custom-call | flops 14680064 | bytes 11010048 | tf_op jit(solution)/shard_map/pallas_call | solution.py:95
  64.9 5.3 %convolution_convert_fusion = bf16[1792,1792]{1,0:T(8,128)(2,1)S(1)} fusion(bf16[512,1792]{1,0:T(8,128)(2,1)S(1)} %copy-done.11, bf16[512,1792]{1,0:T(8,128)(2,1)} %get-tuple-element.30), kind=kOutput, calls=%fused_computation | convolution fusion | flops 3291545600 | bytes 10092544 | tf_op jit(solution)/shard_map/dot_general | solution.py:197
  70.2 2.7 %copy-done.13 = bf16[1792,1792]{1,0:T(8,128)(2,1)} copy-done((bf16[1792,1792]{1,0:T(8,128)(2,1)}, bf16[1792,1792]{1,0:T(8,128)(2,1)S(1)}, u32[]{:S(2)}) %copy-start.13) | copy-done | bytes 6422552
  74.7 4.5 %collective-permute-start.13 = (bf16[448,640]{1,0:T(8,128)(2,1)S(1)}, bf16[448,640]{1,0:T(8,128)(2,1)}, u32[]{:S(2)}, u32[]{:S(2)}) collective-permute-start(bf16[448,640]{1,0:T(8,128)(2,1)S(1)} %get-tuple-element.63), channel_id=1, source_target_pairs={{0,2},{1,3},{8,10},{9,11},{16,18},{17,19},{24,26},{25,27}} | collective-permute-start | bytes 1720328 | tf_op jit(solution)/shard_map/ppermute | solution.py:133
  79.3 2.5 %slice.8 = bf16[1792,1152]{1,0:T(8,128)(2,1)S(1)} slice(bf16[1792,1792]{1,0:T(8,128)(2,1)} %copy-done.13), slice={[0:1792], [0:1152]} | slice | bytes 8257536 | tf_op jit(solution)/shard_map/slice | solution.py:151
  81.8 2.0 copy-done.12
  87.2 16.6 %collective-permute-done.13 = bf16[448,640]{1,0:T(8,128)(2,1)} collective-permute-done((bf16[448,640]{1,0:T(8,128)(2,1)S(1)}, bf16[448,640]{1,0:T(8,128)(2,1)}, u32[]{:S(2)}, u32[]{:S(2)}) %collective-permute-start.13) | collective-permute-done | bytes 573472 | tf_op jit(solution)/shard_map/ppermute | solution.py:133
  103.8 2.5 %fusion.1 = (bf16[448,640]{1,0:T(8,128)(2,1)}, bf16[448,640]{1,0:T(8,128)(2,1)}) fusion(bf16[448,640]{1,0:T(8,128)(2,1)} %collective-permute-done.14, bf16[1792,640]{1,0:T(8,128)(2,1)S(1)} %slice.9, s32[]{:T(128)S(6)} %select_n.142, bf16[448,640]{1,0:T(8,128)(2,1)} %collective-permute-done.13), kind=kLoop, calls=%fused_computation.8 | loop fusion | flops 2007040 | bytes 2867204 | tf_op jit(solution)/shard_map/convert_element_type | solution.py:134
  107.8 5.1 %collective-permute-start.15 = (bf16[448,640]{1,0:T(8,128)(2,1)}, bf16[448,640]{1,0:T(8,128)(2,1)}, u32[]{:S(2)}, u32[]{:S(2)}) collective-permute-start(bf16[448,640]{1,0:T(8,128)(2,1)} %get-tuple-element.61), channel_id=1, source_target_pairs={{0,2},{1,3},{2,4},{3,5},{8,10},{9,11},{10,12},{11,13},{16,18},{17,... | collective-permute-start | bytes 1720328 | tf_op jit(solution)/shard_map/ppermute | solution.py:133
  117.0 3.9 %collective-permute-start.6 = (bf16[224,1152]{1,0:T(8,128)(2,1)S(1)}, bf16[224,1152]{1,0:T(8,128)(2,1)S(1)}, u32[]{:S(2)}, u32[]{:S(2)}) collective-permute-start(bf16[224,1152]{1,0:T(8,128)(2,1)S(1)} %get-tuple-element.59), channel_id=1, source_target_pairs={{0,2},{1,3},{8,10},{9,11},{16,18},{17,19},{24,26},{25,27}} | collective-permute-start | bytes 1548296 | tf_op jit(solution)/shard_map/ppermute | solution.py:133
  120.9 11.9 %collective-permute-done.15 = bf16[448,640]{1,0:T(8,128)(2,1)} collective-permute-done((bf16[448,640]{1,0:T(8,128)(2,1)}, bf16[448,640]{1,0:T(8,128)(2,1)}, u32[]{:S(2)}, u32[]{:S(2)}) %collective-permute-start.15) | collective-permute-done | bytes 573472 | tf_op jit(solution)/shard_map/ppermute | solution.py:133
  136.6 5.0 %collective-permute-start.17 = (bf16[448,640]{1,0:T(8,128)(2,1)S(1)}, bf16[448,640]{1,0:T(8,128)(2,1)S(1)}, u32[]{:S(2)}, u32[]{:S(2)}) collective-permute-start(bf16[448,640]{1,0:T(8,128)(2,1)S(1)} %add_convert_fusion.2), channel_id=1, source_target_pairs={{0,2},{1,3},{2,4},{3,5},{4,6},{5,7},{8,10},{9,11},{10,12},{11,13},... | collective-permute-start | bytes 1720328 | tf_op jit(solution)/shard_map/ppermute | solution.py:133
  147.7 2.9 %collective-permute-done.18 = bf16[448,640]{1,0:T(8,128)(2,1)S(1)} collective-permute-done((bf16[448,640]{1,0:T(8,128)(2,1)S(1)}, bf16[448,640]{1,0:T(8,128)(2,1)S(1)}, u32[]{:S(2)}, u32[]{:S(2)}) %collective-permute-start.18) | collective-permute-done | bytes 573472 | tf_op jit(solution)/shard_map/ppermute | solution.py:134
  150.6 4.7 %collective-permute-start.8 = (bf16[224,1152]{1,0:T(8,128)(2,1)S(1)}, bf16[224,1152]{1,0:T(8,128)(2,1)S(1)}, u32[]{:S(2)}, u32[]{:S(2)}) collective-permute-start(bf16[224,1152]{1,0:T(8,128)(2,1)S(1)} %get-tuple-element.53), channel_id=1, source_target_pairs={{0,2},{1,3},{2,4},{3,5},{8,10},{9,11},{10,12},{11,13},{16,18},{17,... | collective-permute-start | bytes 1548296 | tf_op jit(solution)/shard_map/ppermute | solution.py:133
  158.1 7.0 %collective-permute-start.21 = (f32[1,4]{1,0:T(1,128)S(1)}, f32[1,4]{1,0:T(1,128)S(1)}, u32[]{:S(2)}, u32[]{:S(2)}) collective-permute-start(f32[1,4]{1,0:T(1,128)S(1)} %bitcast_add_fusion), channel_id=1, source_target_pairs={{0,2},{1,3},{2,0},{3,1},{4,6},{5,7},{6,4},{7,5},{8,10},{9,11},{10,... | collective-permute-start | bytes 56 | tf_op jit(solution)/shard_map/ppermute | solution.py:208
  166.7 4.6 %collective-permute-start.22 = (f32[1,4]{1,0:T(1,128)S(1)}, f32[1,4]{1,0:T(1,128)S(1)}, u32[]{:S(2)}, u32[]{:S(2)}) collective-permute-start(f32[1,4]{1,0:T(1,128)S(1)} %add.264), channel_id=1, source_target_pairs={{0,4},{1,5},{2,6},{3,7},{4,0},{5,1},{6,2},{7,3},{8,12},{9,13},{10,... | collective-permute-start | bytes 56 | tf_op jit(solution)/shard_map/ppermute | solution.py:208
  178.0 4.8 %collective-permute-start.10 = (bf16[224,1152]{1,0:T(8,128)(2,1)S(1)}, bf16[224,1152]{1,0:T(8,128)(2,1)S(1)}, u32[]{:S(2)}, u32[]{:S(2)}) collective-permute-start(bf16[224,1152]{1,0:T(8,128)(2,1)S(1)} %add_convert_fusion.5), channel_id=1, source_target_pairs={{0,2},{1,3},{2,4},{3,5},{4,6},{5,7},{8,10},{9,11},{10,12},{11,13},... | collective-permute-start | bytes 1548296 | tf_op jit(solution)/shard_map/ppermute | solution.py:133
  182.8 6.4 %convolution_convert_fusion.1.g_ref = bf16[512,1792]{1,0:T(8,128)(2,1)S(1)} fusion(bf16[512,1792]{1,0:T(8,128)(2,1)S(1)} %copy-done.21, bf16[1792,1792]{1,0:T(8,128)(2,1)} %bitcast.34), kind=kOutput, calls=%fused_computation.1 | convolution fusion | flops 3289251840 | bytes 10092544 | tf_op jit(solution)/shard_map/dot_general | solution.py:212
  189.2 23.9 %shard_map.120 = (bf16[512,1792]{1,0:T(8,128)(2,1)}, bf16[512,1792]{1,0:T(8,128)(2,1)}, bf16[512,1792]{1,0:T(8,128)(2,1)}) custom-call(bf16[512,1792]{1,0:T(8,128)(2,1)S(1)} %bitcast.28, bf16[512,1792]{1,0:T(8,128)(2,1)S(1)} %bitcast.30, bf16[512,1792]{1,0:T(8,128)(2,1)S(1)} %bitcast.32, bf16[512,1792]{1,0:T(8,128)(2,1)S(1)} %convolution_convert_fusion.1.g_ref), custom_call_target="tpu_custom_call" | custom-call | flops 2818572288 | bytes 12845056 | tf_op jit(solution)/shard_map/pallas_call | solution.py:59
  (98 shorter events, 41.1 us)
Async XLA Ops:
  7.2 167.7 %all-gather.2.cloned.1.call-start = ((), (), s32[]{:S(2)}) async-start(), calls=%async_computation | async-start | bytes 7225344 | tf_op jit(solution)/shard_map/all_gather | solution.py:188
  7.9 43.4 %collective-permute-start = (bf16[512,1792]{1,0:T(8,128)(2,1)}, bf16[512,1792]{1,0:T(8,128)(2,1)}, u32[]{:S(2)}, u32[]{:S(2)}) collective-permute-start(bf16[512,1792]{1,0:T(8,128)(2,1)} %bitcast.24), channel_id=1, source_target_pairs={{0,16},{8,24},{16,0},{24,8},{1,17},{9,25},{17,1},{25,9},{2,18},{10... | collective-permute-start | bytes 5505032 | tf_op jit(solution)/shard_map/ppermute | solution.py:174
  10.9 40.8 %collective-permute-start.1 = (bf16[512,1792]{1,0:T(8,128)(2,1)}, bf16[512,1792]{1,0:T(8,128)(2,1)}, u32[]{:S(2)}, u32[]{:S(2)}) collective-permute-start(bf16[512,1792]{1,0:T(8,128)(2,1)} %bitcast.25), channel_id=1, source_target_pairs={{0,8},{8,0},{16,24},{24,16},{1,9},{9,1},{17,25},{25,17},{2,10},{10... | collective-permute-start | bytes 5505032 | tf_op jit(solution)/shard_map/ppermute | solution.py:176
  51.3 4.1 %collective-permute-start.2 = (bf16[512,1792]{1,0:T(8,128)(2,1)}, bf16[512,1792]{1,0:T(8,128)(2,1)}, u32[]{:S(2)}, u32[]{:S(2)}) collective-permute-start(bf16[512,1792]{1,0:T(8,128)(2,1)} %collective-permute-done.refs_1_), channel_id=1, source_target_pairs={{0,8},{8,0},{16,24},{24,16},{1,9},{9,1},{17,25},{25,17},{2,10},{10... | collective-permute-start | bytes 5505032 | tf_op jit(solution)/shard_map/ppermute | solution.py:179
  73.2 14.0 %collective-permute-start.14 = (bf16[448,640]{1,0:T(8,128)(2,1)S(1)}, bf16[448,640]{1,0:T(8,128)(2,1)}, u32[]{:S(2)}, u32[]{:S(2)}) collective-permute-start(bf16[448,640]{1,0:T(8,128)(2,1)S(1)} %get-tuple-element.62), channel_id=1, source_target_pairs={{6,4},{7,5},{14,12},{15,13},{22,20},{23,21},{30,28},{31,29}} | collective-permute-start | bytes 1720328 | tf_op jit(solution)/shard_map/ppermute | solution.py:134
  74.7 29.1 %collective-permute-start.13 = (bf16[448,640]{1,0:T(8,128)(2,1)S(1)}, bf16[448,640]{1,0:T(8,128)(2,1)}, u32[]{:S(2)}, u32[]{:S(2)}) collective-permute-start(bf16[448,640]{1,0:T(8,128)(2,1)S(1)} %get-tuple-element.63), channel_id=1, source_target_pairs={{0,2},{1,3},{8,10},{9,11},{16,18},{17,19},{24,26},{25,27}} | collective-permute-start | bytes 1720328 | tf_op jit(solution)/shard_map/ppermute | solution.py:133
  85.2 29.3 %collective-permute-start.5 = (bf16[224,1152]{1,0:T(8,128)(2,1)}, bf16[224,1152]{1,0:T(8,128)(2,1)}, u32[]{:S(2)}, u32[]{:S(2)}) collective-permute-start(bf16[224,1152]{1,0:T(8,128)(2,1)} %get-tuple-element.55), channel_id=1, source_target_pairs={{0,1},{1,0},{2,3},{3,2},{4,5},{5,4},{6,7},{7,6},{8,9},{9,8},{10,11... | collective-permute-start | bytes 1548296 | tf_op jit(solution)/shard_map/ppermute | solution.py:121
  86.7 27.9 %collective-permute-start.3 = (bf16[224,1152]{1,0:T(8,128)(2,1)}, bf16[224,1152]{1,0:T(8,128)(2,1)}, u32[]{:S(2)}, u32[]{:S(2)}) collective-permute-start(bf16[224,1152]{1,0:T(8,128)(2,1)} %get-tuple-element.57), channel_id=1, source_target_pairs={{0,1},{1,0},{2,3},{3,2},{4,5},{5,4},{6,7},{7,6},{8,9},{9,8},{10,11... | collective-permute-start | bytes 1548296 | tf_op jit(solution)/shard_map/ppermute | solution.py:121
  106.3 14.6 %collective-permute-start.16 = (bf16[448,640]{1,0:T(8,128)(2,1)}, bf16[448,640]{1,0:T(8,128)(2,1)}, u32[]{:S(2)}, u32[]{:S(2)}) collective-permute-start(bf16[448,640]{1,0:T(8,128)(2,1)} %get-tuple-element.60), channel_id=1, source_target_pairs={{4,2},{5,3},{6,4},{7,5},{12,10},{13,11},{14,12},{15,13},{20,18},{2... | collective-permute-start | bytes 1720328 | tf_op jit(solution)/shard_map/ppermute | solution.py:134
  107.8 25.1 %collective-permute-start.15 = (bf16[448,640]{1,0:T(8,128)(2,1)}, bf16[448,640]{1,0:T(8,128)(2,1)}, u32[]{:S(2)}, u32[]{:S(2)}) collective-permute-start(bf16[448,640]{1,0:T(8,128)(2,1)} %get-tuple-element.61), channel_id=1, source_target_pairs={{0,2},{1,3},{2,4},{3,5},{8,10},{9,11},{10,12},{11,13},{16,18},{17,... | collective-permute-start | bytes 1720328 | tf_op jit(solution)/shard_map/ppermute | solution.py:133
  112.9 32.6 %collective-permute-start.4 = (bf16[224,1152]{1,0:T(8,128)(2,1)}, bf16[224,1152]{1,0:T(8,128)(2,1)}, u32[]{:S(2)}, u32[]{:S(2)}) collective-permute-start(bf16[224,1152]{1,0:T(8,128)(2,1)} %get-tuple-element.56), channel_id=1, source_target_pairs={{0,1},{1,0},{2,3},{3,2},{4,5},{5,4},{6,7},{7,6},{8,9},{9,8},{10,11... | collective-permute-start | bytes 1548296 | tf_op jit(solution)/shard_map/ppermute | solution.py:121
  116.3 25.5 %collective-permute-start.7 = (bf16[224,1152]{1,0:T(8,128)(2,1)S(1)}, bf16[224,1152]{1,0:T(8,128)(2,1)S(1)}, u32[]{:S(2)}, u32[]{:S(2)}) collective-permute-start(bf16[224,1152]{1,0:T(8,128)(2,1)S(1)} %get-tuple-element.58), channel_id=1, source_target_pairs={{6,4},{7,5},{14,12},{15,13},{22,20},{23,21},{30,28},{31,29}} | collective-permute-start | bytes 1548296 | tf_op jit(solution)/shard_map/ppermute | solution.py:134
  117.0 26.8 %collective-permute-start.6 = (bf16[224,1152]{1,0:T(8,128)(2,1)S(1)}, bf16[224,1152]{1,0:T(8,128)(2,1)S(1)}, u32[]{:S(2)}, u32[]{:S(2)}) collective-permute-start(bf16[224,1152]{1,0:T(8,128)(2,1)S(1)} %get-tuple-element.59), channel_id=1, source_target_pairs={{0,2},{1,3},{8,10},{9,11},{16,18},{17,19},{24,26},{25,27}} | collective-permute-start | bytes 1548296 | tf_op jit(solution)/shard_map/ppermute | solution.py:133
  134.1 16.5 %collective-permute-start.18 = (bf16[448,640]{1,0:T(8,128)(2,1)S(1)}, bf16[448,640]{1,0:T(8,128)(2,1)S(1)}, u32[]{:S(2)}, u32[]{:S(2)}) collective-permute-start(bf16[448,640]{1,0:T(8,128)(2,1)S(1)} %add_convert_fusion.1), channel_id=1, source_target_pairs={{2,0},{3,1},{4,2},{5,3},{6,4},{7,5},{10,8},{11,9},{12,10},{13,11},... | collective-permute-start | bytes 1720328 | tf_op jit(solution)/shard_map/ppermute | solution.py:134
  136.6 19.5 %collective-permute-start.17 = (bf16[448,640]{1,0:T(8,128)(2,1)S(1)}, bf16[448,640]{1,0:T(8,128)(2,1)S(1)}, u32[]{:S(2)}, u32[]{:S(2)}) collective-permute-start(bf16[448,640]{1,0:T(8,128)(2,1)S(1)} %add_convert_fusion.2), channel_id=1, source_target_pairs={{0,2},{1,3},{2,4},{3,5},{4,6},{5,7},{8,10},{9,11},{10,12},{11,13},... | collective-permute-start | bytes 1720328 | tf_op jit(solution)/shard_map/ppermute | solution.py:133
  141.8 16.4 %collective-permute-start.20 = (f32[1,4]{1,0:T(1,128)S(1)}, f32[1,4]{1,0:T(1,128)S(1)}, u32[]{:S(2)}, u32[]{:S(2)}) collective-permute-start(f32[1,4]{1,0:T(1,128)S(1)} %bitcast.36), channel_id=1, source_target_pairs={{0,1},{1,0},{2,3},{3,2},{4,5},{5,4},{6,7},{7,6},{8,9},{9,8},{10,11... | collective-permute-start | bytes 56 | tf_op jit(solution)/shard_map/ppermute | solution.py:208
  143.8 69.3 %collective-permute-start.12 = (bf16[224,1152]{1,0:T(8,128)(2,1)}, bf16[224,1152]{1,0:T(8,128)(2,1)S(1)}, u32[]{:S(2)}, u32[]{:S(2)}) collective-permute-start(bf16[224,1152]{1,0:T(8,128)(2,1)} %get-tuple-element.54), channel_id=1, source_target_pairs={{0,1},{1,0},{2,3},{3,2},{4,5},{5,4},{6,7},{7,6},{8,9},{9,8},{10,11... | collective-permute-start | bytes 1548296 | tf_op jit(solution)/shard_map/ppermute | solution.py:121
  147.0 26.3 %collective-permute-start.9 = (bf16[224,1152]{1,0:T(8,128)(2,1)S(1)}, bf16[224,1152]{1,0:T(8,128)(2,1)S(1)}, u32[]{:S(2)}, u32[]{:S(2)}) collective-permute-start(bf16[224,1152]{1,0:T(8,128)(2,1)S(1)} %get-tuple-element.52), channel_id=1, source_target_pairs={{4,2},{5,3},{6,4},{7,5},{12,10},{13,11},{14,12},{15,13},{20,18},{2... | collective-permute-start | bytes 1548296 | tf_op jit(solution)/shard_map/ppermute | solution.py:134
  150.6 22.7 %collective-permute-start.8 = (bf16[224,1152]{1,0:T(8,128)(2,1)S(1)}, bf16[224,1152]{1,0:T(8,128)(2,1)S(1)}, u32[]{:S(2)}, u32[]{:S(2)}) collective-permute-start(bf16[224,1152]{1,0:T(8,128)(2,1)S(1)} %get-tuple-element.53), channel_id=1, source_target_pairs={{0,2},{1,3},{2,4},{3,5},{8,10},{9,11},{10,12},{11,13},{16,18},{17,... | collective-permute-start | bytes 1548296 | tf_op jit(solution)/shard_map/ppermute | solution.py:133
  156.4 17.7 %collective-permute-start.19 = (bf16[224,640]{1,0:T(8,128)(2,1)S(1)}, bf16[224,640]{1,0:T(8,128)(2,1)S(1)}, u32[]{:S(2)}, u32[]{:S(2)}) collective-permute-start(bf16[224,640]{1,0:T(8,128)(2,1)S(1)} %constant_dynamic-slice_fusion), channel_id=1, source_target_pairs={{0,1},{1,0},{2,3},{3,2},{4,5},{5,4},{6,7},{7,6},{8,9},{9,8},{10,11... | collective-permute-start | bytes 860168 | tf_op jit(solution)/shard_map/ppermute | solution.py:121
  158.1 8.5 %collective-permute-start.21 = (f32[1,4]{1,0:T(1,128)S(1)}, f32[1,4]{1,0:T(1,128)S(1)}, u32[]{:S(2)}, u32[]{:S(2)}) collective-permute-start(f32[1,4]{1,0:T(1,128)S(1)} %bitcast_add_fusion), channel_id=1, source_target_pairs={{0,2},{1,3},{2,0},{3,1},{4,6},{5,7},{6,4},{7,5},{8,10},{9,11},{10,... | collective-permute-start | bytes 56 | tf_op jit(solution)/shard_map/ppermute | solution.py:208
  166.7 6.1 %collective-permute-start.22 = (f32[1,4]{1,0:T(1,128)S(1)}, f32[1,4]{1,0:T(1,128)S(1)}, u32[]{:S(2)}, u32[]{:S(2)}) collective-permute-start(f32[1,4]{1,0:T(1,128)S(1)} %add.264), channel_id=1, source_target_pairs={{0,4},{1,5},{2,6},{3,7},{4,0},{5,1},{6,2},{7,3},{8,12},{9,13},{10,... | collective-permute-start | bytes 56 | tf_op jit(solution)/shard_map/ppermute | solution.py:208
  176.5 36.6 %collective-permute-start.11 = (bf16[224,1152]{1,0:T(8,128)(2,1)S(1)}, bf16[224,1152]{1,0:T(8,128)(2,1)S(1)}, u32[]{:S(2)}, u32[]{:S(2)}) collective-permute-start(bf16[224,1152]{1,0:T(8,128)(2,1)S(1)} %add_convert_fusion.4), channel_id=1, source_target_pairs={{2,0},{3,1},{4,2},{5,3},{6,4},{7,5},{10,8},{11,9},{12,10},{13,11},... | collective-permute-start | bytes 1548296 | tf_op jit(solution)/shard_map/ppermute | solution.py:134
  178.0 35.1 %collective-permute-start.10 = (bf16[224,1152]{1,0:T(8,128)(2,1)S(1)}, bf16[224,1152]{1,0:T(8,128)(2,1)S(1)}, u32[]{:S(2)}, u32[]{:S(2)}) collective-permute-start(bf16[224,1152]{1,0:T(8,128)(2,1)S(1)} %add_convert_fusion.5), channel_id=1, source_target_pairs={{0,2},{1,3},{2,4},{3,5},{4,6},{5,7},{8,10},{9,11},{10,12},{11,13},... | collective-permute-start | bytes 1548296 | tf_op jit(solution)/shard_map/ppermute | solution.py:133
  (22 other events, 261.5 us)
Sparse Core Ops, SparseCore 0:
  10.2 117.5 all-gather.1

commit v2 on v1

--- a/solution.py
+++ b/solution.py
@@ -16,7 +16,7 @@
 CORES = 2
 VMEM = 40 * 1024 * 1024
 OUTER = 4
-EARLY_X = 1152
+PERMUTED = 1280
 
 
 def dot(a, b, ca, cb):
@@ -139,29 +139,23 @@
     return wide(block_at(0)), right, left
 
 
-def scatter_sum(share, shards, then):
+def scatter_sum(share, shards, sums, then):
     rows = share.shape[0] // shards
     inner = shards // OUTER
     place = lax.axis_index("fsdp")
     far, near = place // inner, place % inner
 
-    def rows_of(array, start, size):
-        return lax.dynamic_slice_in_dim(array, start * rows, size * rows, 0)
-
-    first, second = share[:, :EARLY_X], share[:, EARLY_X:]
-    parts = [
-        sum_inner(
-            lambda i, o=(far + shift) % OUTER: rows_of(first, o * inner + i, 1), inner, near, shards
-        ).astype(jnp.bfloat16)
-        for shift in range(OUTER)
-    ]
-
-    own, right, left = sum_outer(
-        lambda shift: rows_of(second, (far + shift) % OUTER * inner, inner), inner, shards
-    )
-    line = (own + wide(right) + wide(left)).astype(jnp.bfloat16)
-    second_sum = sum_inner(lambda i: rows_of(line, i, 1), inner, near, shards)
-    return second_sum, sum_outer(lambda shift: parts[shift], inner, shards, then)
+    def block(outer, i):
+        return lax.dynamic_slice_in_dim(share, (outer * inner + i) * rows, rows, 0)
+
+    parts = [None] * OUTER
+    for shift in (1, 3, 2, 0):
+        outer = (far + shift) % OUTER
+        parts[shift] = sum_inner(functools.partial(block, outer), inner, near, shards).astype(
+            jnp.bfloat16
+        )
+    parts[2], sums = lax.optimization_barrier((parts[2], sums))
+    return sums, sum_outer(lambda shift: parts[shift], inner, shards, then)
 
 
 def tower_pieces(piece, towers, tower, before):
@@ -194,19 +188,20 @@
     coefs = jnp.sum(jnp.where(here, column[None, :], 0.0), axis=1)[None, :]
 
     residual, dots = stitch_call(coefs, block_out[0], pieces)
-    share = lax.dot_general(
-        attended, residual, (((0,), (0,)), ((), ())), preferred_element_type=jnp.float32
-    ).astype(jnp.bfloat16)
-    held = [weight]
-    second_sum, (own, right, left) = scatter_sum(share, count_shards, held)
-    (weight,) = held
-
+    share, rest = [
+        dot(attended, part, 0, 0).astype(jnp.bfloat16)
+        for part in (residual[:, :PERMUTED], residual[:, PERMUTED:])
+    ]
     sums = jnp.sum(dots, axis=1)
     sums = jnp.sum(jnp.where(here, sums[:, None], 0.0), axis=0)[None, :]
     hop = 1
     while hop < count_shards:
         sums = sums + lax.ppermute(sums, "fsdp", [(d, d ^ hop) for d in range(count_shards)])
         hop *= 2
+    held = [weight]
+    sums, (own, right, left) = scatter_sum(share, count_shards, sums, held)
+    weight, rest = lax.optimization_barrier((held[0], rest))
+    rest = lax.psum_scatter(rest, "fsdp", scatter_dimension=0, tiled=True)
     stitch_grad = sums / (tok_rows * count_shards)
 
     attended_grad = lax.dot_general(
@@ -218,7 +213,7 @@
     right, left, query_out, key_out, value_out = lax.optimization_barrier(
         (right, left, query_out, key_out, value_out)
     )
-    proj_grad = jnp.concatenate([own + wide(right) + wide(left), second_sum], axis=1)
+    proj_grad = jnp.concatenate([own + wide(right) + wide(left), wide(rest)], axis=1)
     return (
         residual[None],
         query_out[None],

time: 223 us -> 254 us (1.14)
  waiting for transfers between devices: 59 us -> 121 us
  starting transfers between devices: 58.5 us -> 34.1 us
  local copies, waits for them, and re-layouts: 18.4 us -> 10.4 us
  matrix products: 11.7 us -> 14.3 us
    ppermute x5 -> x4, waiting for transfers between devices: 0.01 us -> 53.9 us  [sum_inner(): total += wide(lax.ppermute(block_for((mine + shift) % inner), 'fsdp', perm))]
    reduce_scatter x0 -> x1, waiting for transfers between devices: none -> 27.7 us  [body(): rest = lax.psum_scatter(rest, 'fsdp', scatter_dimension=0, tiled=True)]
    ppermute x6 -> x3, waiting for transfers between devices: 29.6 us -> 4.82 us  [sum_outer(): right = lax.ppermute(ahead.astype(jnp.bfloat16), 'fsdp', up)]
    ppermute x6 -> x3, starting transfers between devices: 28.1 us -> 16.6 us  [sum_outer(): right = lax.ppermute(ahead.astype(jnp.bfloat16), 'fsdp', up)]
    ppermute x3, starting transfers between devices: 13.2 us -> 5.53 us  [body(): lax.ppermute(sums, 'fsdp', [(d, d ^ hop) for d in range(count_shards)])]
    ppermute x3, waiting for transfers between devices: 3.08 us -> 10.8 us  [body(): lax.ppermute(sums, 'fsdp', [(d, d ^ hop) for d in range(count_shards)])]
    unnamed x44 -> x26, local copies, waits for them, and re-layouts: 14 us -> 8.87 us
    ppermute x6 -> x3, waiting for transfers between devices: 2.95 us -> 0.01 us  [sum_outer(): left = lax.ppermute(behind.astype(jnp.bfloat16), 'fsdp', down)]
  transfers between devices with their start and end apart: 24 -> 18, of which waited for: 9 -> 10; matrix products, arithmetic and copies ran while one was open for 12% -> 10% of each run, Pallas kernels for 21% -> 19%
where the time goes in v2:
time: 254 us; the launch traced here: 253 us
  waiting for transfers between devices  121 us (48%)
  Pallas kernels  47.1 us (19%)
  starting transfers between devices  34.1 us (13%)
  matrix products  14.3 us (6%)
  between operations  14.2 us (6%)
  other arithmetic  12.2 us (5%)
  local copies, waits for them, and re-layouts  10.4 us (4%)
    ppermute x4, waiting for transfers between devices, sum_inner(): total += wide(lax.ppermute(block_for((mine + shift) % inner), 'fsdp', perm))  53.9 us
    pallas_call x2, Pallas kernels, attention_call(): pl.pallas_call(kernel, grid=(rows // PATCHES, features // width), in_spec...  39.5 us
    reduce_scatter x1, waiting for transfers between devices, body(): rest = lax.psum_scatter(rest, 'fsdp', scatter_dimension=0, tiled=True)  27.7 us
    ppermute x1, waiting for transfers between devices, tower_pieces(): same.append(lax.ppermute(piece, 'task', perm))  19 us
    ppermute x3, starting transfers between devices, sum_outer(): right = lax.ppermute(ahead.astype(jnp.bfloat16), 'fsdp', up)  16.6 us
    ppermute x3, waiting for transfers between devices, body(): lax.ppermute(sums, 'fsdp', [(d, d ^ hop) for d in range(count_shards)])  10.8 us
    unnamed x26, local copies, waits for them, and re-layouts  8.87 us
    pallas_call x1, Pallas kernels, stitch_call(): pl.pallas_call(functools.partial(stitch_kernel, towers), grid=(rows // st...  7.6 us
  transfers between devices with their start and end apart: 18, of which 10 were waited for; matrix products, arithmetic and copies ran while one was open for 10% of the time, Pallas kernels for 19%

profile of v2, /device:TPU:0, one launch (start us, length us, event | category | flops | bytes accessed | tf_op | source)
XLA Modules:
  0.0 252.9 jit_solution(3018472773026581788)
XLA Ops:
  8.0 3.0 %collective-permute-start = (bf16[512,1792]{1,0:T(8,128)(2,1)}, bf16[512,1792]{1,0:T(8,128)(2,1)}, u32[]{:S(2)}, u32[]{:S(2)}) collective-permute-start(bf16[512,1792]{1,0:T(8,128)(2,1)} %bitcast.24), channel_id=1, source_target_pairs={{0,16},{8,24},{16,0},{24,8},{1,17},{9,25},{17,1},{25,9},{2,18},{10... | collective-permute-start | bytes 5505032 | tf_op jit(solution)/shard_map/ppermute | solution.py:168
  15.5 15.6 %shard_map.118 = bf16[512,1792]{1,0:T(8,128)(2,1)S(1)} custom-call(bf16[512,1792]{1,0:T(8,128)(2,1)S(1)} %bitcast.27, bf16[512,1792]{1,0:T(8,128)(2,1)S(1)} %bitcast.29, bf16[512,1792]{1,0:T(8,128)(2,1)S(1)} %bitcast.31), custom_call_target="tpu_custom_call" | custom-call | flops 939524096 | bytes 7340032 | tf_op jit(solution)/shard_map/pallas_call | solution.py:59
  32.4 19.0 %collective-permute-done.refs_1_ = bf16[512,1792]{1,0:T(8,128)(2,1)} collective-permute-done((bf16[512,1792]{1,0:T(8,128)(2,1)}, bf16[512,1792]{1,0:T(8,128)(2,1)}, u32[]{:S(2)}, u32[]{:S(2)}) %collective-permute-start) | collective-permute-done | bytes 1835040 | tf_op jit(solution)/shard_map/ppermute | solution.py:168
  51.8 3.7 %collective-permute-done.2.refs_3_ = bf16[512,1792]{1,0:T(8,128)(2,1)} collective-permute-done((bf16[512,1792]{1,0:T(8,128)(2,1)}, bf16[512,1792]{1,0:T(8,128)(2,1)}, u32[]{:S(2)}, u32[]{:S(2)}) %collective-permute-start.2) | collective-permute-done | bytes 1835040 | tf_op jit(solution)/shard_map/ppermute | solution.py:173
  55.5 1.9 copy-done.2
  57.4 7.6 %shard_map.119 = (bf16[512,1792]{1,0:T(8,128)(2,1)}, f32[4,1792]{1,0:T(4,128)S(1)}) custom-call(f32[1,4]{1,0:T(1,128)S(1)} %bitcast.33, bf16[512,1792]{1,0:T(8,128)(2,1)S(1)} %bitcast.23, bf16[512,1792]{1,0:T(8,128)(2,1)S(1)} %bitcast.26, bf16[512,1792]{1,0:T(8,128)(2,1)} %collective-permute-done.refs_1_, bf16[512,1792]{1,0:T(8,128)(2,1)} %collective-permute-done.1.refs_2_, ...), custom_call_target="tpu_custom_call" | custom-call | flops 14680064 | bytes 11010048 | tf_op jit(solution)/shard_map/pallas_call | solution.py:95
  65.0 3.9 %convolution_convert_fusion = bf16[1792,1280]{1,0:T(8,128)(2,1)S(1)} fusion(bf16[512,1792]{1,0:T(8,128)(2,1)S(1)} %copy-done.10, bf16[512,1792]{1,0:T(8,128)(2,1)} %get-tuple-element.30), kind=kOutput, calls=%fused_computation | convolution fusion | flops 2351104000 | bytes 7733248 | tf_op jit(solution)/shard_map/dot_general | solution.py:23
  71.4 1.8 collective-permute-start.3
  75.2 24.5 %collective-permute-done.3 = bf16[224,1280]{1,0:T(8,128)(2,1)S(1)} collective-permute-done((bf16[224,1280]{1,0:T(8,128)(2,1)}, bf16[224,1280]{1,0:T(8,128)(2,1)S(1)}, u32[]{:S(2)}, u32[]{:S(2)}) %collective-permute-start.3) | collective-permute-done | bytes 573472 | tf_op jit(solution)/shard_map/ppermute | solution.py:121
  99.7 17.4 %collective-permute-done.8 = bf16[224,1280]{1,0:T(8,128)(2,1)S(1)} collective-permute-done((bf16[224,1280]{1,0:T(8,128)(2,1)S(1)}, bf16[224,1280]{1,0:T(8,128)(2,1)S(1)}, u32[]{:S(2)}, u32[]{:S(2)}) %collective-permute-start.8) | collective-permute-done | bytes 573472 | tf_op jit(solution)/shard_map/ppermute | solution.py:121
  117.1 12.0 %collective-permute-done.4 = bf16[224,1280]{1,0:T(8,128)(2,1)S(1)} collective-permute-done((bf16[224,1280]{1,0:T(8,128)(2,1)S(1)}, bf16[224,1280]{1,0:T(8,128)(2,1)S(1)}, u32[]{:S(2)}, u32[]{:S(2)}) %collective-permute-start.4) | collective-permute-done | bytes 573472 | tf_op jit(solution)/shard_map/ppermute | solution.py:121
  129.2 2.6 %add_convert_fusion.5 = (bf16[224,1280]{1,0:T(8,128)(2,1)S(1)}, bf16[224,1280]{1,0:T(8,128)(2,1)S(1)}, bf16[224,1280]{1,0:T(8,128)(2,1)}) fusion(bf16[224,1280]{1,0:T(8,128)(2,1)S(1)} %collective-permute-done.3, bf16[1792,1280]{1,0:T(8,128)(2,1)} %copy-done.12, s32[]{:T(128)S(6)} %select_n.91, bf16[224,1280]{1,0:T(8,128)(2,1)S(1)} %collective-permute-done.8, ...), kind=kLoop, calls=%fused_computation.15 | loop fusion | flops 3440640 | bytes 5160972 | tf_op jit(solution)/shard_map/convert_element_type | solution.py:154
  131.8 4.3 %collective-permute-start.9 = (bf16[224,1280]{1,0:T(8,128)(2,1)S(1)}, bf16[224,1280]{1,0:T(8,128)(2,1)}, u32[]{:S(2)}, u32[]{:S(2)}) collective-permute-start(bf16[224,1280]{1,0:T(8,128)(2,1)S(1)} %get-tuple-element.57), channel_id=1, source_target_pairs={{0,2},{1,3},{8,10},{9,11},{16,18},{17,19},{24,26},{25,27}} | collective-permute-start | bytes 1720328 | tf_op jit(solution)/shard_map/ppermute | solution.py:133
  138.4 3.0 %collective-permute-done.5 = f32[1,4]{1,0:T(1,128)S(1)} collective-permute-done((f32[1,4]{1,0:T(1,128)S(1)}, f32[1,4]{1,0:T(1,128)S(1)}, u32[]{:S(2)}, u32[]{:S(2)}) %collective-permute-start.5) | collective-permute-done | bytes 48 | tf_op jit(solution)/shard_map/ppermute | solution.py:199
  141.4 6.3 %collective-permute-done.6 = f32[1,4]{1,0:T(1,128)S(1)} collective-permute-done((f32[1,4]{1,0:T(1,128)S(1)}, f32[1,4]{1,0:T(1,128)S(1)}, u32[]{:S(2)}, u32[]{:S(2)}) %collective-permute-start.6) | collective-permute-done | bytes 48 | tf_op jit(solution)/shard_map/ppermute | solution.py:199
  147.7 4.9 %collective-permute-start.7 = (f32[1,4]{1,0:T(1,128)S(1)}, f32[1,4]{1,0:T(1,128)S(1)}, u32[]{:S(2)}, u32[]{:S(2)}) collective-permute-start(f32[1,4]{1,0:T(1,128)S(1)} %add.177), channel_id=1, source_target_pairs={{0,4},{1,5},{2,6},{3,7},{4,0},{5,1},{6,2},{7,3},{8,12},{9,13},{10,... | collective-permute-start | bytes 56 | tf_op jit(solution)/shard_map/ppermute | solution.py:199
  154.2 2.6 %fusion.2 = (bf16[224,1280]{1,0:T(8,128)(2,1)}, bf16[224,1280]{1,0:T(8,128)(2,1)}) fusion(bf16[224,1280]{1,0:T(8,128)(2,1)} %get-tuple-element.33, bf16[224,1280]{1,0:T(8,128)(2,1)} %collective-permute-done.10, bf16[224,1280]{1,0:T(8,128)(2,1)} %collective-permute-done.9), kind=kLoop, calls=%fused_computation.8 | loop fusion | flops 2007040 | bytes 2867200 | tf_op jit(solution)/shard_map/convert_element_type | solution.py:134
  156.8 3.2 %collective-permute-start.11 = (bf16[224,1280]{1,0:T(8,128)(2,1)}, bf16[224,1280]{1,0:T(8,128)(2,1)}, u32[]{:S(2)}, u32[]{:S(2)}) collective-permute-start(bf16[224,1280]{1,0:T(8,128)(2,1)} %get-tuple-element.60), channel_id=1, source_target_pairs={{0,2},{1,3},{2,4},{3,5},{8,10},{9,11},{10,12},{11,13},{16,18},{17,... | collective-permute-start | bytes 1720328 | tf_op jit(solution)/shard_map/ppermute | solution.py:133
  161.5 3.5 %convolution_convert_fusion.2 = bf16[1792,512]{1,0:T(8,128)(2,1)} fusion(bf16[512,1792]{1,0:T(8,128)(2,1)S(1)} %copy-done.11, bf16[512,1792]{1,0:T(8,128)(2,1)} %get-tuple-element.30), kind=kOutput, calls=%fused_computation.2 | convolution fusion | flops 940441600 | bytes 4194304 | tf_op jit(solution)/shard_map/dot_general | solution.py:23
  165.0 4.8 %collective-permute-done.11 = bf16[224,1280]{1,0:T(8,128)(2,1)} collective-permute-done((bf16[224,1280]{1,0:T(8,128)(2,1)}, bf16[224,1280]{1,0:T(8,128)(2,1)}, u32[]{:S(2)}, u32[]{:S(2)}) %collective-permute-start.11) | collective-permute-done | bytes 573472 | tf_op jit(solution)/shard_map/ppermute | solution.py:133
  172.0 9.0 %collective-permute-start.13 = (bf16[224,1280]{1,0:T(8,128)(2,1)S(1)}, bf16[224,1280]{1,0:T(8,128)(2,1)S(1)}, u32[]{:S(2)}, u32[]{:S(2)}) collective-permute-start(bf16[224,1280]{1,0:T(8,128)(2,1)S(1)} %add_convert_fusion.2), channel_id=1, source_target_pairs={{0,2},{1,3},{2,4},{3,5},{4,6},{5,7},{8,10},{9,11},{10,12},{11,13},... | collective-permute-start | bytes 1720328 | tf_op jit(solution)/shard_map/ppermute | solution.py:133
  184.0 6.9 %convolution_convert_fusion.1.g_ref = bf16[512,1792]{1,0:T(8,128)(2,1)S(1)} fusion(bf16[512,1792]{1,0:T(8,128)(2,1)} %get-tuple-element.30, bf16[1792,1792]{1,0:T(8,128)(2,1)} %bitcast.34), kind=kOutput, calls=%fused_computation.1 | convolution fusion | flops 3289251840 | bytes 10092544 | tf_op jit(solution)/shard_map/dot_general | solution.py:207
  191.0 23.9 %shard_map.120 = (bf16[512,1792]{1,0:T(8,128)(2,1)}, bf16[512,1792]{1,0:T(8,128)(2,1)}, bf16[512,1792]{1,0:T(8,128)(2,1)}) custom-call(bf16[512,1792]{1,0:T(8,128)(2,1)S(1)} %bitcast.28, bf16[512,1792]{1,0:T(8,128)(2,1)S(1)} %bitcast.30, bf16[512,1792]{1,0:T(8,128)(2,1)S(1)} %bitcast.32, bf16[512,1792]{1,0:T(8,128)(2,1)S(1)} %convolution_convert_fusion.1.g_ref), custom_call_target="tpu_custom_call" | custom-call | flops 2818572288 | bytes 12845056 | tf_op jit(solution)/shard_map/pallas_call | solution.py:59
  216.2 27.7 %reduce-scatter.2.cloned.1.call-done = bf16[224,512]{1,0:T(8,128)(2,1)} async-done(((bf16[1792,512]{1,0:T(8,128)(2,1)}), bf16[224,512]{1,0:T(8,128)(2,1)}) %reduce-scatter.2.cloned.1.call-update) | async-done | bytes 229392 | tf_op jit(solution)/shard_map/reduce_scatter | solution.py:204
  (63 shorter events, 25.5 us)
Async XLA Ops:
  7.2 44.2 %copy-start = (f32[4,4]{1,0:T(4,128)S(1)}, f32[4,4]{1,0:T(4,128)}, u32[]{:S(2)}) copy-start(f32[4,4]{1,0:T(4,128)} %param.7) | copy-start | bytes 196
  7.2 162.7 %all-gather.2.cloned.1.call-start = ((), (), s32[]{:S(2)}) async-start(), calls=%async_computation.1 | async-start | bytes 7225344 | tf_op jit(solution)/shard_map/all_gather | solution.py:182
  7.9 235.9 %reduce-scatter.2.cloned.1.call-start = ((), (), s32[]{:S(2)}) async-start(), calls=%async_computation.2 | async-start | bytes 2064384 | tf_op jit(solution)/shard_map/reduce_scatter | solution.py:204
  8.0 43.4 %collective-permute-start = (bf16[512,1792]{1,0:T(8,128)(2,1)}, bf16[512,1792]{1,0:T(8,128)(2,1)}, u32[]{:S(2)}, u32[]{:S(2)}) collective-permute-start(bf16[512,1792]{1,0:T(8,128)(2,1)} %bitcast.24), channel_id=1, source_target_pairs={{0,16},{8,24},{16,0},{24,8},{1,17},{9,25},{17,1},{25,9},{2,18},{10... | collective-permute-start | bytes 5505032 | tf_op jit(solution)/shard_map/ppermute | solution.py:168
  11.0 40.8 %collective-permute-start.1 = (bf16[512,1792]{1,0:T(8,128)(2,1)}, bf16[512,1792]{1,0:T(8,128)(2,1)}, u32[]{:S(2)}, u32[]{:S(2)}) collective-permute-start(bf16[512,1792]{1,0:T(8,128)(2,1)} %bitcast.25), channel_id=1, source_target_pairs={{0,8},{8,0},{16,24},{24,16},{1,9},{9,1},{17,25},{25,17},{2,10},{10... | collective-permute-start | bytes 5505032 | tf_op jit(solution)/shard_map/ppermute | solution.py:170
  15.5 40.0 %copy-start.1 = (bf16[1,512,1792]{2,1,0:T(8,128)(2,1)S(1)}, bf16[1,512,1792]{2,1,0:T(8,128)(2,1)}, u32[]{:S(2)}) copy-start(bf16[1,512,1792]{2,1,0:T(8,128)(2,1)} %param.9) | copy-start | bytes 5505028
  51.3 4.1 %collective-permute-start.2 = (bf16[512,1792]{1,0:T(8,128)(2,1)}, bf16[512,1792]{1,0:T(8,128)(2,1)}, u32[]{:S(2)}, u32[]{:S(2)}) collective-permute-start(bf16[512,1792]{1,0:T(8,128)(2,1)} %collective-permute-done.refs_1_), channel_id=1, source_target_pairs={{0,8},{8,0},{16,24},{24,16},{1,9},{9,1},{17,25},{25,17},{2,10},{10... | collective-permute-start | bytes 5505032 | tf_op jit(solution)/shard_map/ppermute | solution.py:173
  71.4 28.3 %collective-permute-start.3 = (bf16[224,1280]{1,0:T(8,128)(2,1)}, bf16[224,1280]{1,0:T(8,128)(2,1)S(1)}, u32[]{:S(2)}, u32[]{:S(2)}) collective-permute-start(bf16[224,1280]{1,0:T(8,128)(2,1)} %get-tuple-element.55), channel_id=1, source_target_pairs={{0,1},{1,0},{2,3},{3,2},{4,5},{5,4},{6,7},{7,6},{8,9},{9,8},{10,11... | collective-permute-start | bytes 1720328 | tf_op jit(solution)/shard_map/ppermute | solution.py:121
  73.2 43.9 %collective-permute-start.8 = (bf16[224,1280]{1,0:T(8,128)(2,1)S(1)}, bf16[224,1280]{1,0:T(8,128)(2,1)S(1)}, u32[]{:S(2)}, u32[]{:S(2)}) collective-permute-start(bf16[224,1280]{1,0:T(8,128)(2,1)S(1)} %get-tuple-element.53), channel_id=1, source_target_pairs={{0,1},{1,0},{2,3},{3,2},{4,5},{5,4},{6,7},{7,6},{8,9},{9,8},{10,11... | collective-permute-start | bytes 1720328 | tf_op jit(solution)/shard_map/ppermute | solution.py:121
  73.5 55.7 %collective-permute-start.4 = (bf16[224,1280]{1,0:T(8,128)(2,1)S(1)}, bf16[224,1280]{1,0:T(8,128)(2,1)S(1)}, u32[]{:S(2)}, u32[]{:S(2)}) collective-permute-start(bf16[224,1280]{1,0:T(8,128)(2,1)S(1)} %get-tuple-element.54), channel_id=1, source_target_pairs={{0,1},{1,0},{2,3},{3,2},{4,5},{5,4},{6,7},{7,6},{8,9},{9,8},{10,11... | collective-permute-start | bytes 1720328 | tf_op jit(solution)/shard_map/ppermute | solution.py:121
  131.8 29.8 %copy-start.11 = (bf16[512,1792]{1,0:T(8,128)(2,1)S(1)}, bf16[512,1792]{1,0:T(8,128)(2,1)}, u32[]{:S(2)}) copy-start(bf16[512,1792]{1,0:T(8,128)(2,1)} %copy-done.9) | copy-start | bytes 5505028
  131.8 22.4 %collective-permute-start.9 = (bf16[224,1280]{1,0:T(8,128)(2,1)S(1)}, bf16[224,1280]{1,0:T(8,128)(2,1)}, u32[]{:S(2)}, u32[]{:S(2)}) collective-permute-start(bf16[224,1280]{1,0:T(8,128)(2,1)S(1)} %get-tuple-element.57), channel_id=1, source_target_pairs={{0,2},{1,3},{8,10},{9,11},{16,18},{17,19},{24,26},{25,27}} | collective-permute-start | bytes 1720328 | tf_op jit(solution)/shard_map/ppermute | solution.py:133
  136.1 18.0 %collective-permute-start.10 = (bf16[224,1280]{1,0:T(8,128)(2,1)S(1)}, bf16[224,1280]{1,0:T(8,128)(2,1)}, u32[]{:S(2)}, u32[]{:S(2)}) collective-permute-start(bf16[224,1280]{1,0:T(8,128)(2,1)S(1)} %get-tuple-element.56), channel_id=1, source_target_pairs={{6,4},{7,5},{14,12},{15,13},{22,20},{23,21},{30,28},{31,29}} | collective-permute-start | bytes 1720328 | tf_op jit(solution)/shard_map/ppermute | solution.py:134
  137.8 3.6 %collective-permute-start.5 = (f32[1,4]{1,0:T(1,128)S(1)}, f32[1,4]{1,0:T(1,128)S(1)}, u32[]{:S(2)}, u32[]{:S(2)}) collective-permute-start(f32[1,4]{1,0:T(1,128)S(1)} %bitcast.36), channel_id=1, source_target_pairs={{0,1},{1,0},{2,3},{3,2},{4,5},{5,4},{6,7},{7,6},{8,9},{9,8},{10,11... | collective-permute-start | bytes 56 | tf_op jit(solution)/shard_map/ppermute | solution.py:199
  141.4 6.3 %collective-permute-start.6 = (f32[1,4]{1,0:T(1,128)S(1)}, f32[1,4]{1,0:T(1,128)S(1)}, u32[]{:S(2)}, u32[]{:S(2)}) collective-permute-start(f32[1,4]{1,0:T(1,128)S(1)} %bitcast_add_fusion), channel_id=1, source_target_pairs={{0,2},{1,3},{2,0},{3,1},{4,6},{5,7},{6,4},{7,5},{8,10},{9,11},{10,... | collective-permute-start | bytes 56 | tf_op jit(solution)/shard_map/ppermute | solution.py:199
  147.7 6.5 %collective-permute-start.7 = (f32[1,4]{1,0:T(1,128)S(1)}, f32[1,4]{1,0:T(1,128)S(1)}, u32[]{:S(2)}, u32[]{:S(2)}) collective-permute-start(f32[1,4]{1,0:T(1,128)S(1)} %add.177), channel_id=1, source_target_pairs={{0,4},{1,5},{2,6},{3,7},{4,0},{5,1},{6,2},{7,3},{8,12},{9,13},{10,... | collective-permute-start | bytes 56 | tf_op jit(solution)/shard_map/ppermute | solution.py:199
  156.8 13.1 %collective-permute-start.11 = (bf16[224,1280]{1,0:T(8,128)(2,1)}, bf16[224,1280]{1,0:T(8,128)(2,1)}, u32[]{:S(2)}, u32[]{:S(2)}) collective-permute-start(bf16[224,1280]{1,0:T(8,128)(2,1)} %get-tuple-element.60), channel_id=1, source_target_pairs={{0,2},{1,3},{2,4},{3,5},{8,10},{9,11},{10,12},{11,13},{16,18},{17,... | collective-permute-start | bytes 1720328 | tf_op jit(solution)/shard_map/ppermute | solution.py:133
  160.0 9.8 %collective-permute-start.12 = (bf16[224,1280]{1,0:T(8,128)(2,1)}, bf16[224,1280]{1,0:T(8,128)(2,1)}, u32[]{:S(2)}, u32[]{:S(2)}) collective-permute-start(bf16[224,1280]{1,0:T(8,128)(2,1)} %get-tuple-element.59), channel_id=1, source_target_pairs={{4,2},{5,3},{6,4},{7,5},{12,10},{13,11},{14,12},{15,13},{20,18},{2... | collective-permute-start | bytes 1720328 | tf_op jit(solution)/shard_map/ppermute | solution.py:134
  169.9 44.9 %collective-permute-start.15 = (bf16[224,1280]{1,0:T(8,128)(2,1)}, bf16[224,1280]{1,0:T(8,128)(2,1)S(1)}, u32[]{:S(2)}, u32[]{:S(2)}) collective-permute-start(bf16[224,1280]{1,0:T(8,128)(2,1)} %get-tuple-element.52), channel_id=1, source_target_pairs={{0,1},{1,0},{2,3},{3,2},{4,5},{5,4},{6,7},{7,6},{8,9},{9,8},{10,11... | collective-permute-start | bytes 1720328 | tf_op jit(solution)/shard_map/ppermute | solution.py:121
  172.0 42.8 %collective-permute-start.13 = (bf16[224,1280]{1,0:T(8,128)(2,1)S(1)}, bf16[224,1280]{1,0:T(8,128)(2,1)S(1)}, u32[]{:S(2)}, u32[]{:S(2)}) collective-permute-start(bf16[224,1280]{1,0:T(8,128)(2,1)S(1)} %add_convert_fusion.2), channel_id=1, source_target_pairs={{0,2},{1,3},{2,4},{3,5},{4,6},{5,7},{8,10},{9,11},{10,12},{11,13},... | collective-permute-start | bytes 1720328 | tf_op jit(solution)/shard_map/ppermute | solution.py:133
  182.2 8.7 %copy-start.4 = (bf16[1,512,1792]{2,1,0:T(8,128)(2,1)S(1)}, bf16[1,512,1792]{2,1,0:T(8,128)(2,1)}, u32[]{:S(2)}) copy-start(bf16[1,512,1792]{2,1,0:T(8,128)(2,1)} %param.10) | copy-start | bytes 5505028
  182.2 8.7 %copy-start.6 = (bf16[1,512,1792]{2,1,0:T(8,128)(2,1)S(1)}, bf16[1,512,1792]{2,1,0:T(8,128)(2,1)}, u32[]{:S(2)}) copy-start(bf16[1,512,1792]{2,1,0:T(8,128)(2,1)} %param.11) | copy-start | bytes 5505028
  182.2 8.7 %copy-start.8 = (bf16[1,512,1792]{2,1,0:T(8,128)(2,1)S(1)}, bf16[1,512,1792]{2,1,0:T(8,128)(2,1)}, u32[]{:S(2)}) copy-start(bf16[1,512,1792]{2,1,0:T(8,128)(2,1)} %param.12) | copy-start | bytes 5505028
  182.3 32.6 %collective-permute-start.14 = (bf16[224,1280]{1,0:T(8,128)(2,1)S(1)}, bf16[224,1280]{1,0:T(8,128)(2,1)S(1)}, u32[]{:S(2)}, u32[]{:S(2)}) collective-permute-start(bf16[224,1280]{1,0:T(8,128)(2,1)S(1)} %add_convert_fusion.1), channel_id=1, source_target_pairs={{2,0},{3,1},{4,2},{5,3},{6,4},{7,5},{10,8},{11,9},{12,10},{13,11},... | collective-permute-start | bytes 1720328 | tf_op jit(solution)/shard_map/ppermute | solution.py:134
  (7 other events, 17.8 us)
Sparse Core Ops, SparseCore 0:
  10.2 120.3 all-gather.1
  170.0 73.8 reduce-scatter.1

commit v3 on v1

--- a/solution.py
+++ b/solution.py
@@ -122,7 +122,7 @@
     return total
 
 
-def sum_outer(block_at, inner, shards, then=None):
+def sum_outer(block_at, inner, shards, then=None, early=None):
     right = left = None
     for far in range(OUTER - 1, 0, -1):
         ahead, behind = wide(block_at(far)), wide(block_at(OUTER - far))
@@ -134,12 +134,14 @@
         left = lax.ppermute(behind.astype(jnp.bfloat16), "fsdp", down)
         if far > 1:
             right, left = lax.optimization_barrier((right, left))
+        if far == OUTER - 1 and early is not None:
+            right, left, *early[:] = lax.optimization_barrier((right, left, *early))
         if far == 2 and then is not None:
             right, left, *then[:] = lax.optimization_barrier((right, left, *then))
     return wide(block_at(0)), right, left
 
 
-def scatter_sum(share, shards, then):
+def scatter_sum(share, shards, then, early):
     rows = share.shape[0] // shards
     inner = shards // OUTER
     place = lax.axis_index("fsdp")
@@ -157,7 +159,7 @@
     ]
 
     own, right, left = sum_outer(
-        lambda shift: rows_of(second, (far + shift) % OUTER * inner, inner), inner, shards
+        lambda shift: rows_of(second, (far + shift) % OUTER * inner, inner), inner, shards, early=early
     )
     line = (own + wide(right) + wide(left)).astype(jnp.bfloat16)
     second_sum = sum_inner(lambda i: rows_of(line, i, 1), inner, near, shards)
@@ -197,17 +199,17 @@
     share = lax.dot_general(
         attended, residual, (((0,), (0,)), ((), ())), preferred_element_type=jnp.float32
     ).astype(jnp.bfloat16)
-    held = [weight]
-    second_sum, (own, right, left) = scatter_sum(share, count_shards, held)
-    (weight,) = held
-
     sums = jnp.sum(dots, axis=1)
     sums = jnp.sum(jnp.where(here, sums[:, None], 0.0), axis=0)[None, :]
     hop = 1
     while hop < count_shards:
         sums = sums + lax.ppermute(sums, "fsdp", [(d, d ^ hop) for d in range(count_shards)])
         hop *= 2
-    stitch_grad = sums / (tok_rows * count_shards)
+    held, early = [weight], [sums]
+    second_sum, (own, right, left) = scatter_sum(share, count_shards, held, early)
+    (weight,) = held
+
+    stitch_grad = early[0] / (tok_rows * count_shards)
 
     attended_grad = lax.dot_general(
         residual, weight, (((1,), (1,)), ((), ())), preferred_element_type=jnp.float32

time: 223 us -> 218 us (0.978)
  starting transfers between devices: 58.5 us -> 49.2 us
  waiting for transfers between devices: 59 us -> 62.8 us
  local copies, waits for them, and re-layouts: 18.4 us -> 15.6 us
  other arithmetic: 13.6 us -> 16.2 us
    ppermute x3, waiting for transfers between devices: 3.08 us -> 19.7 us  [body(): lax.ppermute(sums, 'fsdp', [(d, d ^ hop) for d in range(count_shards)])]
    ppermute x6, waiting for transfers between devices: 29.6 us -> 18.9 us  [sum_outer(): right = lax.ppermute(ahead.astype(jnp.bfloat16), 'fsdp', up)]
    ppermute x3, starting transfers between devices: 13.2 us -> 4.34 us  [body(): lax.ppermute(sums, 'fsdp', [(d, d ^ hop) for d in range(count_shards)])]
    ppermute x6, waiting for transfers between devices: 2.95 us -> 0.02 us  [sum_outer(): left = lax.ppermute(behind.astype(jnp.bfloat16), 'fsdp', down)]
    unnamed x44 -> x32, local copies, waits for them, and re-layouts: 14 us -> 11.3 us
  transfers between devices with their start and end apart: 24 -> 24, of which waited for: 9 -> 9; matrix products, arithmetic and copies ran while one was open for 12% -> 14% of each run, Pallas kernels for 21% -> 22%
where the time goes in v3:
time: 218 us; the launch traced here: 217 us
  waiting for transfers between devices  62.8 us (29%)
  starting transfers between devices  49.2 us (23%)
  Pallas kernels  47.1 us (22%)
  other arithmetic  16.2 us (7%)
  local copies, waits for them, and re-layouts  15.6 us (7%)
  between operations  14.4 us (7%)
  matrix products  11.7 us (5%)
    pallas_call x2, Pallas kernels, attention_call(): pl.pallas_call(kernel, grid=(rows // PATCHES, features // width), in_spec...  39.5 us
    ppermute x6, starting transfers between devices, sum_outer(): right = lax.ppermute(ahead.astype(jnp.bfloat16), 'fsdp', up)  29 us
    ppermute x3, waiting for transfers between devices, body(): lax.ppermute(sums, 'fsdp', [(d, d ^ hop) for d in range(count_shards)])  19.7 us
    ppermute x1, waiting for transfers between devices, tower_pieces(): same.append(lax.ppermute(piece, 'task', perm))  19 us
    ppermute x6, waiting for transfers between devices, sum_outer(): right = lax.ppermute(ahead.astype(jnp.bfloat16), 'fsdp', up)  18.9 us
    unnamed x32, local copies, waits for them, and re-layouts  11.3 us
    pallas_call x1, Pallas kernels, stitch_call(): pl.pallas_call(functools.partial(stitch_kernel, towers), grid=(rows // st...  7.59 us
    ppermute x6, starting transfers between devices, sum_outer(): left = lax.ppermute(behind.astype(jnp.bfloat16), 'fsdp', down)  7.13 us
  transfers between devices with their start and end apart: 24, of which 9 were waited for; matrix products, arithmetic and copies ran while one was open for 14% of the time, Pallas kernels for 22%

profile of v3, /device:TPU:0, one launch (start us, length us, event | category | flops | bytes accessed | tf_op | source)
XLA Modules:
  0.0 216.8 jit_solution(14615325331115055836)
XLA Ops:
  7.9 3.0 %collective-permute-start = (bf16[512,1792]{1,0:T(8,128)(2,1)}, bf16[512,1792]{1,0:T(8,128)(2,1)}, u32[]{:S(2)}, u32[]{:S(2)}) collective-permute-start(bf16[512,1792]{1,0:T(8,128)(2,1)} %bitcast.24), channel_id=1, source_target_pairs={{0,16},{8,24},{16,0},{24,8},{1,17},{9,25},{17,1},{25,9},{2,18},{10... | collective-permute-start | bytes 5505032 | tf_op jit(solution)/shard_map/ppermute | solution.py:176
  15.5 15.6 %shard_map.118 = bf16[512,1792]{1,0:T(8,128)(2,1)S(1)} custom-call(bf16[512,1792]{1,0:T(8,128)(2,1)S(1)} %bitcast.27, bf16[512,1792]{1,0:T(8,128)(2,1)S(1)} %bitcast.29, bf16[512,1792]{1,0:T(8,128)(2,1)S(1)} %bitcast.31), custom_call_target="tpu_custom_call" | custom-call | flops 939524096 | bytes 7340032 | tf_op jit(solution)/shard_map/pallas_call | solution.py:59
  32.3 19.0 %collective-permute-done.refs_1_ = bf16[512,1792]{1,0:T(8,128)(2,1)} collective-permute-done((bf16[512,1792]{1,0:T(8,128)(2,1)}, bf16[512,1792]{1,0:T(8,128)(2,1)}, u32[]{:S(2)}, u32[]{:S(2)}) %collective-permute-start) | collective-permute-done | bytes 1835040 | tf_op jit(solution)/shard_map/ppermute | solution.py:176
  51.7 3.7 %collective-permute-done.2.refs_3_ = bf16[512,1792]{1,0:T(8,128)(2,1)} collective-permute-done((bf16[512,1792]{1,0:T(8,128)(2,1)}, bf16[512,1792]{1,0:T(8,128)(2,1)}, u32[]{:S(2)}, u32[]{:S(2)}) %collective-permute-start.2) | collective-permute-done | bytes 1835040 | tf_op jit(solution)/shard_map/ppermute | solution.py:181
  57.3 7.6 %shard_map.119 = (bf16[512,1792]{1,0:T(8,128)(2,1)}, f32[4,1792]{1,0:T(4,128)S(1)}) custom-call(f32[1,4]{1,0:T(1,128)S(1)} %bitcast.33, bf16[512,1792]{1,0:T(8,128)(2,1)S(1)} %bitcast.23, bf16[512,1792]{1,0:T(8,128)(2,1)S(1)} %bitcast.26, bf16[512,1792]{1,0:T(8,128)(2,1)} %collective-permute-done.refs_1_, bf16[512,1792]{1,0:T(8,128)(2,1)} %collective-permute-done.1.refs_2_, ...), custom_call_target="tpu_custom_call" | custom-call | flops 14680064 | bytes 11010048 | tf_op jit(solution)/shard_map/pallas_call | solution.py:95
  64.9 5.3 %convolution_convert_fusion = bf16[1792,1792]{1,0:T(8,128)(2,1)S(1)} fusion(bf16[512,1792]{1,0:T(8,128)(2,1)S(1)} %copy-done.11, bf16[512,1792]{1,0:T(8,128)(2,1)} %get-tuple-element.33), kind=kOutput, calls=%fused_computation | convolution fusion | flops 3291545600 | bytes 10092544 | tf_op jit(solution)/shard_map/dot_general | solution.py:199
  74.3 3.8 %collective-permute-start.13 = (bf16[448,640]{1,0:T(8,128)(2,1)S(1)}, bf16[448,640]{1,0:T(8,128)(2,1)S(1)}, u32[]{:S(2)}, u32[]{:S(2)}) collective-permute-start(bf16[448,640]{1,0:T(8,128)(2,1)S(1)} %get-tuple-element.69), channel_id=1, source_target_pairs={{0,2},{1,3},{8,10},{9,11},{16,18},{17,19},{24,26},{25,27}} | collective-permute-start | bytes 1720328 | tf_op jit(solution)/shard_map/ppermute | solution.py:133
  78.3 2.5 %slice.8 = bf16[1792,1152]{1,0:T(8,128)(2,1)S(1)} slice(bf16[1792,1792]{1,0:T(8,128)(2,1)} %copy-done.14), slice={[0:1792], [0:1152]} | slice | bytes 8257536 | tf_op jit(solution)/shard_map/slice | solution.py:153
  86.2 17.2 %collective-permute-done.16 = f32[1,4]{1,0:T(1,128)S(1)} collective-permute-done((f32[1,4]{1,0:T(1,128)S(1)}, f32[1,4]{1,0:T(1,128)S(1)}, u32[]{:S(2)}, u32[]{:S(2)}) %collective-permute-start.16) | collective-permute-done | bytes 48 | tf_op jit(solution)/shard_map/ppermute | solution.py:206
  103.4 2.8 %collective-permute-start.17 = (f32[1,4]{1,0:T(1,128)S(1)}, f32[1,4]{1,0:T(1,128)S(1)}, u32[]{:S(2)}, u32[]{:S(2)}) collective-permute-start(f32[1,4]{1,0:T(1,128)S(1)} %add.255), channel_id=1, source_target_pairs={{0,4},{1,5},{2,6},{3,7},{4,0},{5,1},{6,2},{7,3},{8,12},{9,13},{10,... | collective-permute-start | bytes 56 | tf_op jit(solution)/shard_map/ppermute | solution.py:206
  106.2 2.5 %collective-permute-done.17 = f32[1,4]{1,0:T(1,128)S(1)} collective-permute-done((f32[1,4]{1,0:T(1,128)S(1)}, f32[1,4]{1,0:T(1,128)S(1)}, u32[]{:S(2)}, u32[]{:S(2)}) %collective-permute-start.17) | collective-permute-done | bytes 48 | tf_op jit(solution)/shard_map/ppermute | solution.py:206
  108.7 2.1 fusion.1
  111.6 5.0 %collective-permute-start.18 = (bf16[448,640]{1,0:T(8,128)(2,1)S(1)}, bf16[448,640]{1,0:T(8,128)(2,1)}, u32[]{:S(2)}, u32[]{:S(2)}) collective-permute-start(bf16[448,640]{1,0:T(8,128)(2,1)S(1)} %get-tuple-element.67), channel_id=1, source_target_pairs={{0,2},{1,3},{2,4},{3,5},{8,10},{9,11},{10,12},{11,13},{16,18},{17,... | collective-permute-start | bytes 1720328 | tf_op jit(solution)/shard_map/ppermute | solution.py:133
  121.3 4.6 %collective-permute-start.6 = (bf16[224,1152]{1,0:T(8,128)(2,1)S(1)}, bf16[224,1152]{1,0:T(8,128)(2,1)}, u32[]{:S(2)}, u32[]{:S(2)}) collective-permute-start(bf16[224,1152]{1,0:T(8,128)(2,1)S(1)} %get-tuple-element.65), channel_id=1, source_target_pairs={{0,2},{1,3},{8,10},{9,11},{16,18},{17,19},{24,26},{25,27}} | collective-permute-start | bytes 1548296 | tf_op jit(solution)/shard_map/ppermute | solution.py:133
  125.9 7.1 %collective-permute-done.18 = bf16[448,640]{1,0:T(8,128)(2,1)} collective-permute-done((bf16[448,640]{1,0:T(8,128)(2,1)S(1)}, bf16[448,640]{1,0:T(8,128)(2,1)}, u32[]{:S(2)}, u32[]{:S(2)}) %collective-permute-start.18) | collective-permute-done | bytes 573472 | tf_op jit(solution)/shard_map/ppermute | solution.py:133
  136.5 5.2 %collective-permute-start.20 = (bf16[448,640]{1,0:T(8,128)(2,1)S(1)}, bf16[448,640]{1,0:T(8,128)(2,1)S(1)}, u32[]{:S(2)}, u32[]{:S(2)}) collective-permute-start(bf16[448,640]{1,0:T(8,128)(2,1)S(1)} %add_convert_fusion.2), channel_id=1, source_target_pairs={{0,2},{1,3},{2,4},{3,5},{4,6},{5,7},{8,10},{9,11},{10,12},{11,13},... | collective-permute-start | bytes 1720328 | tf_op jit(solution)/shard_map/ppermute | solution.py:133
  141.7 2.4 %collective-permute-done.6 = bf16[224,1152]{1,0:T(8,128)(2,1)} collective-permute-done((bf16[224,1152]{1,0:T(8,128)(2,1)S(1)}, bf16[224,1152]{1,0:T(8,128)(2,1)}, u32[]{:S(2)}, u32[]{:S(2)}) %collective-permute-start.6) | collective-permute-done | bytes 516128 | tf_op jit(solution)/shard_map/ppermute | solution.py:133
  144.1 2.7 %fusion.3 = (bf16[224,1152]{1,0:T(8,128)(2,1)}, bf16[224,1152]{1,0:T(8,128)(2,1)}) fusion(bf16[224,1152]{1,0:T(8,128)(2,1)} %collective-permute-done.7, bf16[224,1152]{1,0:T(8,128)(2,1)} %collective-permute-done.4, bf16[1792,1152]{1,0:T(8,128)(2,1)} %copy-done.12, s32[]{:T(128)S(6)} %select_n.132, bf16[224,1152]{1,0:T(8,128)(2,1)} %collective-permute-done.6), kind=kLoop, calls=%fused_computation.13 | loop fusion | flops 2838528 | bytes 3096580 | tf_op jit(solution)/shard_map/convert_element_type | solution.py:134
  148.3 5.2 %collective-permute-start.8 = (bf16[224,1152]{1,0:T(8,128)(2,1)}, bf16[224,1152]{1,0:T(8,128)(2,1)}, u32[]{:S(2)}, u32[]{:S(2)}) collective-permute-start(bf16[224,1152]{1,0:T(8,128)(2,1)} %get-tuple-element.59), channel_id=1, source_target_pairs={{0,2},{1,3},{2,4},{3,5},{8,10},{9,11},{10,12},{11,13},{16,18},{17,... | collective-permute-start | bytes 1548296 | tf_op jit(solution)/shard_map/ppermute | solution.py:133
  153.4 3.0 %collective-permute-done.20 = bf16[448,640]{1,0:T(8,128)(2,1)S(1)} collective-permute-done((bf16[448,640]{1,0:T(8,128)(2,1)S(1)}, bf16[448,640]{1,0:T(8,128)(2,1)S(1)}, u32[]{:S(2)}, u32[]{:S(2)}) %collective-permute-start.20) | collective-permute-done | bytes 573472 | tf_op jit(solution)/shard_map/ppermute | solution.py:133
  160.3 6.4 %collective-permute-done.8 = bf16[224,1152]{1,0:T(8,128)(2,1)} collective-permute-done((bf16[224,1152]{1,0:T(8,128)(2,1)}, bf16[224,1152]{1,0:T(8,128)(2,1)}, u32[]{:S(2)}, u32[]{:S(2)}) %collective-permute-start.8) | collective-permute-done | bytes 516128 | tf_op jit(solution)/shard_map/ppermute | solution.py:133
  171.8 5.4 %collective-permute-start.10 = (bf16[224,1152]{1,0:T(8,128)(2,1)S(1)}, bf16[224,1152]{1,0:T(8,128)(2,1)S(1)}, u32[]{:S(2)}, u32[]{:S(2)}) collective-permute-start(bf16[224,1152]{1,0:T(8,128)(2,1)S(1)} %add_convert_fusion.5), channel_id=1, source_target_pairs={{0,2},{1,3},{2,4},{3,5},{4,6},{5,7},{8,10},{9,11},{10,12},{11,13},... | collective-permute-start | bytes 1548296 | tf_op jit(solution)/shard_map/ppermute | solution.py:133
  177.1 6.4 %convolution_convert_fusion.1.g_ref = bf16[512,1792]{1,0:T(8,128)(2,1)S(1)} fusion(bf16[512,1792]{1,0:T(8,128)(2,1)S(1)} %copy-done.15, bf16[1792,1792]{1,0:T(8,128)(2,1)} %bitcast.34), kind=kOutput, calls=%fused_computation.1 | convolution fusion | flops 3289251840 | bytes 10092544 | tf_op jit(solution)/shard_map/dot_general | solution.py:214
  183.5 23.9 %shard_map.120 = (bf16[512,1792]{1,0:T(8,128)(2,1)}, bf16[512,1792]{1,0:T(8,128)(2,1)}, bf16[512,1792]{1,0:T(8,128)(2,1)}) custom-call(bf16[512,1792]{1,0:T(8,128)(2,1)S(1)} %bitcast.28, bf16[512,1792]{1,0:T(8,128)(2,1)S(1)} %bitcast.30, bf16[512,1792]{1,0:T(8,128)(2,1)S(1)} %bitcast.32, bf16[512,1792]{1,0:T(8,128)(2,1)S(1)} %convolution_convert_fusion.1.g_ref), custom_call_target="tpu_custom_call" | custom-call | flops 2818572288 | bytes 12845056 | tf_op jit(solution)/shard_map/pallas_call | solution.py:59
  (87 shorter events, 40.3 us)
Async XLA Ops:
  7.2 160.5 %all-gather.2.cloned.1.call-start = ((), (), s32[]{:S(2)}) async-start(), calls=%async_computation | async-start | bytes 7225344 | tf_op jit(solution)/shard_map/all_gather | solution.py:190
  7.9 43.4 %collective-permute-start = (bf16[512,1792]{1,0:T(8,128)(2,1)}, bf16[512,1792]{1,0:T(8,128)(2,1)}, u32[]{:S(2)}, u32[]{:S(2)}) collective-permute-start(bf16[512,1792]{1,0:T(8,128)(2,1)} %bitcast.24), channel_id=1, source_target_pairs={{0,16},{8,24},{16,0},{24,8},{1,17},{9,25},{17,1},{25,9},{2,18},{10... | collective-permute-start | bytes 5505032 | tf_op jit(solution)/shard_map/ppermute | solution.py:176
  10.9 40.8 %collective-permute-start.1 = (bf16[512,1792]{1,0:T(8,128)(2,1)}, bf16[512,1792]{1,0:T(8,128)(2,1)}, u32[]{:S(2)}, u32[]{:S(2)}) collective-permute-start(bf16[512,1792]{1,0:T(8,128)(2,1)} %bitcast.25), channel_id=1, source_target_pairs={{0,8},{8,0},{16,24},{24,16},{1,9},{9,1},{17,25},{25,17},{2,10},{10... | collective-permute-start | bytes 5505032 | tf_op jit(solution)/shard_map/ppermute | solution.py:178
  51.3 4.1 %collective-permute-start.2 = (bf16[512,1792]{1,0:T(8,128)(2,1)}, bf16[512,1792]{1,0:T(8,128)(2,1)}, u32[]{:S(2)}, u32[]{:S(2)}) collective-permute-start(bf16[512,1792]{1,0:T(8,128)(2,1)} %collective-permute-done.refs_1_), channel_id=1, source_target_pairs={{0,8},{8,0},{16,24},{24,16},{1,9},{9,1},{17,25},{25,17},{2,10},{10... | collective-permute-start | bytes 5505032 | tf_op jit(solution)/shard_map/ppermute | solution.py:181
  73.6 35.1 %collective-permute-start.14 = (bf16[448,640]{1,0:T(8,128)(2,1)S(1)}, bf16[448,640]{1,0:T(8,128)(2,1)S(1)}, u32[]{:S(2)}, u32[]{:S(2)}) collective-permute-start(bf16[448,640]{1,0:T(8,128)(2,1)S(1)} %get-tuple-element.68), channel_id=1, source_target_pairs={{6,4},{7,5},{14,12},{15,13},{22,20},{23,21},{30,28},{31,29}} | collective-permute-start | bytes 1720328 | tf_op jit(solution)/shard_map/ppermute | solution.py:134
  74.3 34.4 %collective-permute-start.13 = (bf16[448,640]{1,0:T(8,128)(2,1)S(1)}, bf16[448,640]{1,0:T(8,128)(2,1)S(1)}, u32[]{:S(2)}, u32[]{:S(2)}) collective-permute-start(bf16[448,640]{1,0:T(8,128)(2,1)S(1)} %get-tuple-element.69), channel_id=1, source_target_pairs={{0,2},{1,3},{8,10},{9,11},{16,18},{17,19},{24,26},{25,27}} | collective-permute-start | bytes 1720328 | tf_op jit(solution)/shard_map/ppermute | solution.py:133
  80.8 5.4 %collective-permute-start.15 = (f32[1,4]{1,0:T(1,128)S(1)}, f32[1,4]{1,0:T(1,128)S(1)}, u32[]{:S(2)}, u32[]{:S(2)}) collective-permute-start(f32[1,4]{1,0:T(1,128)S(1)} %bitcast.36), channel_id=1, source_target_pairs={{0,1},{1,0},{2,3},{3,2},{4,5},{5,4},{6,7},{7,6},{8,9},{9,8},{10,11... | collective-permute-start | bytes 56 | tf_op jit(solution)/shard_map/ppermute | solution.py:206
  84.2 33.8 %collective-permute-start.5 = (bf16[224,1152]{1,0:T(8,128)(2,1)}, bf16[224,1152]{1,0:T(8,128)(2,1)}, u32[]{:S(2)}, u32[]{:S(2)}) collective-permute-start(bf16[224,1152]{1,0:T(8,128)(2,1)} %get-tuple-element.61), channel_id=1, source_target_pairs={{0,1},{1,0},{2,3},{3,2},{4,5},{5,4},{6,7},{7,6},{8,9},{9,8},{10,11... | collective-permute-start | bytes 1548296 | tf_op jit(solution)/shard_map/ppermute | solution.py:121
  85.7 32.3 %collective-permute-start.3 = (bf16[224,1152]{1,0:T(8,128)(2,1)}, bf16[224,1152]{1,0:T(8,128)(2,1)}, u32[]{:S(2)}, u32[]{:S(2)}) collective-permute-start(bf16[224,1152]{1,0:T(8,128)(2,1)} %get-tuple-element.63), channel_id=1, source_target_pairs={{0,1},{1,0},{2,3},{3,2},{4,5},{5,4},{6,7},{7,6},{8,9},{9,8},{10,11... | collective-permute-start | bytes 1548296 | tf_op jit(solution)/shard_map/ppermute | solution.py:121
  86.2 17.2 %collective-permute-start.16 = (f32[1,4]{1,0:T(1,128)S(1)}, f32[1,4]{1,0:T(1,128)S(1)}, u32[]{:S(2)}, u32[]{:S(2)}) collective-permute-start(f32[1,4]{1,0:T(1,128)S(1)} %bitcast_add_fusion), channel_id=1, source_target_pairs={{0,2},{1,3},{2,0},{3,1},{4,6},{5,7},{6,4},{7,5},{8,10},{9,11},{10,... | collective-permute-start | bytes 56 | tf_op jit(solution)/shard_map/ppermute | solution.py:206
  103.4 5.3 %collective-permute-start.17 = (f32[1,4]{1,0:T(1,128)S(1)}, f32[1,4]{1,0:T(1,128)S(1)}, u32[]{:S(2)}, u32[]{:S(2)}) collective-permute-start(f32[1,4]{1,0:T(1,128)S(1)} %add.255), channel_id=1, source_target_pairs={{0,4},{1,5},{2,6},{3,7},{4,0},{5,1},{6,2},{7,3},{8,12},{9,13},{10,... | collective-permute-start | bytes 56 | tf_op jit(solution)/shard_map/ppermute | solution.py:206
  110.9 15.0 %collective-permute-start.19 = (bf16[448,640]{1,0:T(8,128)(2,1)}, bf16[448,640]{1,0:T(8,128)(2,1)S(1)}, u32[]{:S(2)}, u32[]{:S(2)}) collective-permute-start(bf16[448,640]{1,0:T(8,128)(2,1)} %get-tuple-element.66), channel_id=1, source_target_pairs={{4,2},{5,3},{6,4},{7,5},{12,10},{13,11},{14,12},{15,13},{20,18},{2... | collective-permute-start | bytes 1720328 | tf_op jit(solution)/shard_map/ppermute | solution.py:134
  111.6 21.4 %collective-permute-start.18 = (bf16[448,640]{1,0:T(8,128)(2,1)S(1)}, bf16[448,640]{1,0:T(8,128)(2,1)}, u32[]{:S(2)}, u32[]{:S(2)}) collective-permute-start(bf16[448,640]{1,0:T(8,128)(2,1)S(1)} %get-tuple-element.67), channel_id=1, source_target_pairs={{0,2},{1,3},{2,4},{3,5},{8,10},{9,11},{10,12},{11,13},{16,18},{17,... | collective-permute-start | bytes 1720328 | tf_op jit(solution)/shard_map/ppermute | solution.py:133
  116.5 27.5 %collective-permute-start.4 = (bf16[224,1152]{1,0:T(8,128)(2,1)}, bf16[224,1152]{1,0:T(8,128)(2,1)}, u32[]{:S(2)}, u32[]{:S(2)}) collective-permute-start(bf16[224,1152]{1,0:T(8,128)(2,1)} %get-tuple-element.62), channel_id=1, source_target_pairs={{0,1},{1,0},{2,3},{3,2},{4,5},{5,4},{6,7},{7,6},{8,9},{9,8},{10,11... | collective-permute-start | bytes 1548296 | tf_op jit(solution)/shard_map/ppermute | solution.py:121
  119.8 21.9 %collective-permute-start.7 = (bf16[224,1152]{1,0:T(8,128)(2,1)S(1)}, bf16[224,1152]{1,0:T(8,128)(2,1)}, u32[]{:S(2)}, u32[]{:S(2)}) collective-permute-start(bf16[224,1152]{1,0:T(8,128)(2,1)S(1)} %get-tuple-element.64), channel_id=1, source_target_pairs={{6,4},{7,5},{14,12},{15,13},{22,20},{23,21},{30,28},{31,29}} | collective-permute-start | bytes 1548296 | tf_op jit(solution)/shard_map/ppermute | solution.py:134
  121.3 22.8 %collective-permute-start.6 = (bf16[224,1152]{1,0:T(8,128)(2,1)S(1)}, bf16[224,1152]{1,0:T(8,128)(2,1)}, u32[]{:S(2)}, u32[]{:S(2)}) collective-permute-start(bf16[224,1152]{1,0:T(8,128)(2,1)S(1)} %get-tuple-element.65), channel_id=1, source_target_pairs={{0,2},{1,3},{8,10},{9,11},{16,18},{17,19},{24,26},{25,27}} | collective-permute-start | bytes 1548296 | tf_op jit(solution)/shard_map/ppermute | solution.py:133
  135.2 18.2 %collective-permute-start.21 = (bf16[448,640]{1,0:T(8,128)(2,1)}, bf16[448,640]{1,0:T(8,128)(2,1)S(1)}, u32[]{:S(2)}, u32[]{:S(2)}) collective-permute-start(bf16[448,640]{1,0:T(8,128)(2,1)} %add_convert_fusion.1), channel_id=1, source_target_pairs={{2,0},{3,1},{4,2},{5,3},{6,4},{7,5},{10,8},{11,9},{12,10},{13,11},... | collective-permute-start | bytes 1720328 | tf_op jit(solution)/shard_map/ppermute | solution.py:134
  136.5 19.9 %collective-permute-start.20 = (bf16[448,640]{1,0:T(8,128)(2,1)S(1)}, bf16[448,640]{1,0:T(8,128)(2,1)S(1)}, u32[]{:S(2)}, u32[]{:S(2)}) collective-permute-start(bf16[448,640]{1,0:T(8,128)(2,1)S(1)} %add_convert_fusion.2), channel_id=1, source_target_pairs={{0,2},{1,3},{2,4},{3,5},{4,6},{5,7},{8,10},{9,11},{10,12},{11,13},... | collective-permute-start | bytes 1720328 | tf_op jit(solution)/shard_map/ppermute | solution.py:133
  146.8 13.5 %collective-permute-start.9 = (bf16[224,1152]{1,0:T(8,128)(2,1)}, bf16[224,1152]{1,0:T(8,128)(2,1)}, u32[]{:S(2)}, u32[]{:S(2)}) collective-permute-start(bf16[224,1152]{1,0:T(8,128)(2,1)} %get-tuple-element.58), channel_id=1, source_target_pairs={{4,2},{5,3},{6,4},{7,5},{12,10},{13,11},{14,12},{15,13},{20,18},{2... | collective-permute-start | bytes 1548296 | tf_op jit(solution)/shard_map/ppermute | solution.py:134
  148.3 18.5 %collective-permute-start.8 = (bf16[224,1152]{1,0:T(8,128)(2,1)}, bf16[224,1152]{1,0:T(8,128)(2,1)}, u32[]{:S(2)}, u32[]{:S(2)}) collective-permute-start(bf16[224,1152]{1,0:T(8,128)(2,1)} %get-tuple-element.59), channel_id=1, source_target_pairs={{0,2},{1,3},{2,4},{3,5},{8,10},{9,11},{10,12},{11,13},{16,18},{17,... | collective-permute-start | bytes 1548296 | tf_op jit(solution)/shard_map/ppermute | solution.py:133
  157.7 9.8 %collective-permute-start.22 = (bf16[224,640]{1,0:T(8,128)(2,1)S(1)}, bf16[224,640]{1,0:T(8,128)(2,1)S(1)}, u32[]{:S(2)}, u32[]{:S(2)}) collective-permute-start(bf16[224,640]{1,0:T(8,128)(2,1)S(1)} %constant_dynamic-slice_fusion), channel_id=1, source_target_pairs={{0,1},{1,0},{2,3},{3,2},{4,5},{5,4},{6,7},{7,6},{8,9},{9,8},{10,11... | collective-permute-start | bytes 860168 | tf_op jit(solution)/shard_map/ppermute | solution.py:121
  159.4 48.0 %collective-permute-start.12 = (bf16[224,1152]{1,0:T(8,128)(2,1)}, bf16[224,1152]{1,0:T(8,128)(2,1)S(1)}, u32[]{:S(2)}, u32[]{:S(2)}) collective-permute-start(bf16[224,1152]{1,0:T(8,128)(2,1)} %get-tuple-element.60), channel_id=1, source_target_pairs={{0,1},{1,0},{2,3},{3,2},{4,5},{5,4},{6,7},{7,6},{8,9},{9,8},{10,11... | collective-permute-start | bytes 1548296 | tf_op jit(solution)/shard_map/ppermute | solution.py:121
  170.2 37.2 %collective-permute-start.11 = (bf16[224,1152]{1,0:T(8,128)(2,1)S(1)}, bf16[224,1152]{1,0:T(8,128)(2,1)S(1)}, u32[]{:S(2)}, u32[]{:S(2)}) collective-permute-start(bf16[224,1152]{1,0:T(8,128)(2,1)S(1)} %add_convert_fusion.4), channel_id=1, source_target_pairs={{2,0},{3,1},{4,2},{5,3},{6,4},{7,5},{10,8},{11,9},{12,10},{13,11},... | collective-permute-start | bytes 1548296 | tf_op jit(solution)/shard_map/ppermute | solution.py:134
  171.8 35.7 %collective-permute-start.10 = (bf16[224,1152]{1,0:T(8,128)(2,1)S(1)}, bf16[224,1152]{1,0:T(8,128)(2,1)S(1)}, u32[]{:S(2)}, u32[]{:S(2)}) collective-permute-start(bf16[224,1152]{1,0:T(8,128)(2,1)S(1)} %add_convert_fusion.5), channel_id=1, source_target_pairs={{0,2},{1,3},{2,4},{3,5},{4,6},{5,7},{8,10},{9,11},{10,12},{11,13},... | collective-permute-start | bytes 1548296 | tf_op jit(solution)/shard_map/ppermute | solution.py:133
  (16 other events, 158.4 us)
Sparse Core Ops, SparseCore 0:
  10.2 114.6 all-gather.1
